TPU v7x, 32 devices: a whole 2x2x4 slice. The times are simulated.
32 devices in a mesh: hi: 8 (over z, x), lo: 4 (over y, core).
Axes of the slice: x: 2, y: 2, z: 4, core: 2. Of those that a mesh axis runs over, the one named last changes fastest.
Arguments:
- sources: bfloat16 [64, 524288], P(None, ('hi', 'lo')), may hold values from -6 to 6
- leaf_in: bfloat16 [2048, 64, 256], P(('hi', 'lo')), may hold values from -0.375 to 0.375
- local_mix: bfloat16 [2048, 6, 64, 128], P(('hi', 'lo')), may hold values from -0.5 to 0.5
- lo_mix: bfloat16 [2048, 2, 64, 128], P(('hi', 'lo')), may hold values from -0.5 to 0.5
- hi_mix: bfloat16 [2048, 3, 64, 128], P(('hi', 'lo')), may hold values from -0.5 to 0.5
- leaf_out: bfloat16 [2048, 64, 256], P(('hi', 'lo')), may hold values from -0.75 to 0.75
Outputs:
- targets: bfloat16 [64, 524288], P(None, ('hi', 'lo'))
All inputs are finite; a program needn't handle non-finite values.
Results may differ from a plain program's by a relative error of at most 0.029.
Values may be sent and summed in bfloat16 or wider, within the bound.
No kernel may reach another device: no remote copies, remote signals or barrier semaphores. Data moves between devices by JAX's collectives and lax.ppermute only.
A program may use at most 128 MiB of HBM per device.

v0:
```python
import jax
import jax.numpy as jnp
from jax import lax
from jax.sharding import PartitionSpec as P


def swapped(block, axis, stride):
    count = lax.axis_size(axis)
    route = []
    for low in range(count):
        high = low | 1 << stride
        if high != low and high < count:
            route += [(low, high), (high, low)]
    return lax.ppermute(block, axis, route)


def flip_blocks(current, level_bit, block_dim):
    shape_now = current.shape
    head_shape = shape_now[:block_dim]
    grouped = current.reshape(
        head_shape
        + (shape_now[block_dim] >> level_bit + 1, 2, 1 << level_bit)
        + shape_now[block_dim + 1 :]
    )
    return lax.rev(grouped, (block_dim + 1,)).reshape(shape_now)


def mix_level(current, partner, factors):
    joined = jnp.concatenate([current, partner], axis=-1)
    mixed = jnp.einsum("kvs,kqs->kvq", joined, factors, preferred_element_type=jnp.float32)
    return mixed.astype(jnp.bfloat16)


def body(sources, leaf_in, local_mix, lo_mix, hi_mix, leaf_out):
    blocks_here = leaf_in.shape[0]
    leaf_size = leaf_in.shape[2]
    vectors = sources.shape[0]
    local_levels = local_mix.shape[1]
    lo_count = lax.axis_size("lo")
    lo_levels = lo_count.bit_length() - 1
    hi_levels = lax.axis_size("hi").bit_length() - 1
    source_blocks = sources.reshape(vectors, blocks_here, leaf_size)
    current = jnp.einsum(
        "vkl,krl->kvr", source_blocks, leaf_in, preferred_element_type=jnp.float32
    ).astype(jnp.bfloat16)
    for level in range(local_levels):
        current = mix_level(current, flip_blocks(current, level, 0), local_mix[:, level])
    for level in range(lo_levels):
        partner = swapped(current, "lo", level)
        current = mix_level(current, partner, lo_mix[:, level])
    for level in range(hi_levels):
        partner = swapped(current, "hi", level)
        current = mix_level(current, partner, hi_mix[:, level])
    result = jnp.einsum("kvr,krl->vkl", current, leaf_out, preferred_element_type=jnp.float32)
    return result.reshape(vectors, blocks_here * leaf_size).astype(jnp.bfloat16)


def solution(mesh):
    return jax.shard_map(
        body,
        mesh=mesh,
        in_specs=(
            P(None, ("hi", "lo")),
            P(("hi", "lo"), None, None),
            P(("hi", "lo"), None, None, None),
            P(("hi", "lo"), None, None, None),
            P(("hi", "lo"), None, None, None),
            P(("hi", "lo"), None, None),
        ),
        out_specs=P(None, ("hi", "lo")),
        check_vma=False,
    )
```

profile of v0, /device:TPU:0, one launch (start us, length us, event | category | flops | bytes accessed | tf_op | source)
XLA Modules:
  0.0 169.3 jit_solution(12749878115398628671)
XLA Ops:
  0.0 0.0 copy-start
  0.0 3.1 %fusion.3 = bf16[64,64,64]{2,1,0:T(8,128)(2,1)S(1)} fusion(bf16[64,64,256]{2,1,0:T(8,128)(2,1)} %param.7, bf16[8,64,8,256]{3,2,1,0:T(8,128)(2,1)} %bitcast.90), kind=kOutput, calls=%fused_computation.4 | convolution fusion | flops 134479872 | bytes 4718592 | tf_op jit(solution)/shard_map/vkl,krl->kvr/dot_general | solution.py:43
  3.1 1.1 rev.18
  4.2 3.3 %convolution_convert_fusion.10 = bf16[64,64,64]{2,1,0:T(8,128)(2,1)} fusion(bf16[64,64,64]{2,1,0:T(8,128)(2,1)} %bitcast.84, bf16[64,64,64]{2,1,0:T(8,128)(2,1)S(1)} %fusion.3, bf16[64,6,64,128]{3,2,1,0:T(8,128)(2,1)} %param.8), kind=kOutput, calls=%fused_computation.15 | convolution fusion | flops 69468160 | bytes 3145728 | tf_op jit(solution)/shard_map/kvs,kqs->kvq/dot_general | solution.py:30
  7.4 0.0 copy-start.1
  7.4 2.4 %rev.19 = bf16[16,2,2,64,64]{4,3,2,1,0:T(8,128)(2,1)} reverse(bf16[16,2,2,64,64]{4,3,2,1,0:T(8,128)(2,1)} %bitcast.79), dimensions={1} | reverse | bytes 1048576 | tf_op jit(solution)/shard_map/rev | solution.py:25
  9.8 0.0 copy-done.1
  9.8 3.3 %convolution_convert_fusion.9 = bf16[64,64,64]{2,1,0:T(8,128)(2,1)} fusion(bf16[64,64,64]{2,1,0:T(8,128)(2,1)} %bitcast.85, bf16[64,64,64]{2,1,0:T(8,128)(2,1)S(1)} %copy-done.1, bf16[64,6,64,128]{3,2,1,0:T(8,128)(2,1)} %param.8), kind=kOutput, calls=%fused_computation.14 | convolution fusion | flops 69468160 | bytes 3145728 | tf_op jit(solution)/shard_map/kvs,kqs->kvq/dot_general | solution.py:30
  13.1 0.0 copy-start.2
  13.1 2.4 %rev.20 = bf16[8,2,4,64,64]{4,3,2,1,0:T(8,128)(2,1)} reverse(bf16[8,2,4,64,64]{4,3,2,1,0:T(8,128)(2,1)} %bitcast.80), dimensions={1} | reverse | bytes 1048576 | tf_op jit(solution)/shard_map/rev | solution.py:25
  15.5 0.0 copy-done.2
  15.5 3.3 %convolution_convert_fusion.8 = bf16[64,64,64]{2,1,0:T(8,128)(2,1)} fusion(bf16[64,64,64]{2,1,0:T(8,128)(2,1)} %bitcast.86, bf16[64,64,64]{2,1,0:T(8,128)(2,1)S(1)} %copy-done.2, bf16[64,6,64,128]{3,2,1,0:T(8,128)(2,1)} %param.8), kind=kOutput, calls=%fused_computation.13 | convolution fusion | flops 69468160 | bytes 3145728 | tf_op jit(solution)/shard_map/kvs,kqs->kvq/dot_general | solution.py:30
  18.7 0.0 copy-start.3
  18.7 2.4 %rev.21 = bf16[4,2,8,64,64]{4,3,2,1,0:T(8,128)(2,1)} reverse(bf16[4,2,8,64,64]{4,3,2,1,0:T(8,128)(2,1)} %bitcast.81), dimensions={1} | reverse | bytes 1048576 | tf_op jit(solution)/shard_map/rev | solution.py:25
  21.1 0.0 copy-done.3
  21.1 3.3 %convolution_convert_fusion.7 = bf16[64,64,64]{2,1,0:T(8,128)(2,1)} fusion(bf16[64,64,64]{2,1,0:T(8,128)(2,1)} %bitcast.87, bf16[64,64,64]{2,1,0:T(8,128)(2,1)S(1)} %copy-done.3, bf16[64,6,64,128]{3,2,1,0:T(8,128)(2,1)} %param.8), kind=kOutput, calls=%fused_computation.12 | convolution fusion | flops 69468160 | bytes 3145728 | tf_op jit(solution)/shard_map/kvs,kqs->kvq/dot_general | solution.py:30
  24.4 0.0 copy-start.4
  24.4 2.4 %rev.22 = bf16[2,2,16,64,64]{4,3,2,1,0:T(8,128)(2,1)} reverse(bf16[2,2,16,64,64]{4,3,2,1,0:T(8,128)(2,1)} %bitcast.82), dimensions={1} | reverse | bytes 1048576 | tf_op jit(solution)/shard_map/rev | solution.py:25
  26.7 0.0 copy-done.4
  26.7 3.3 %convolution_convert_fusion.6 = bf16[64,64,64]{2,1,0:T(8,128)(2,1)} fusion(bf16[64,64,64]{2,1,0:T(8,128)(2,1)} %bitcast.88, bf16[64,64,64]{2,1,0:T(8,128)(2,1)S(1)} %copy-done.4, bf16[64,6,64,128]{3,2,1,0:T(8,128)(2,1)} %param.8), kind=kOutput, calls=%fused_computation.11 | convolution fusion | flops 69468160 | bytes 3145728 | tf_op jit(solution)/shard_map/kvs,kqs->kvq/dot_general | solution.py:30
  30.0 0.0 copy-start.5
  30.0 2.4 %rev.23 = bf16[1,2,32,64,64]{4,3,2,1,0:T(8,128)(2,1)} reverse(bf16[1,2,32,64,64]{4,3,2,1,0:T(8,128)(2,1)} %bitcast.83), dimensions={1} | reverse | bytes 1048576 | tf_op jit(solution)/shard_map/rev | solution.py:25
  32.3 0.0 copy-done.5
  32.3 0.0 copy-start.7
  32.3 2.4 %convolution_convert_fusion.5 = bf16[64,64,64]{2,1,0:T(8,128)(2,1)S(1)} fusion(bf16[64,64,64]{2,1,0:T(8,128)(2,1)} %bitcast.89, bf16[64,64,64]{2,1,0:T(8,128)(2,1)S(1)} %copy-done.5, bf16[64,6,64,128]{3,2,1,0:T(8,128)(2,1)} %param.8), kind=kOutput, calls=%fused_computation.10 | convolution fusion | flops 69468160 | bytes 3145728 | tf_op jit(solution)/shard_map/kvs,kqs->kvq/dot_general | solution.py:30
  34.8 0.5 collective-permute-start
  35.3 2.3 %collective-permute-done = bf16[64,64,64]{2,1,0:T(8,128)(2,1)S(1)} collective-permute-done((bf16[64,64,64]{2,1,0:T(8,128)(2,1)S(1)}, bf16[64,64,64]{2,1,0:T(8,128)(2,1)S(1)}, u32[]{:S(2)}, u32[]{:S(2)}) %collective-permute-start) | collective-permute-done | bytes 524320 | tf_op jit(solution)/shard_map/ppermute | solution.py:14
  37.6 0.0 copy-done.7
  37.6 0.7 convolution_convert_fusion.4
  38.3 0.0 copy-start.6
  38.4 3.0 %collective-permute-start.1 = (bf16[64,64,64]{2,1,0:T(8,128)(2,1)S(1)}, bf16[64,64,64]{2,1,0:T(8,128)(2,1)S(1)}, u32[]{:S(2)}, u32[]{:S(2)}) collective-permute-start(bf16[64,64,64]{2,1,0:T(8,128)(2,1)S(1)} %convolution_convert_fusion.4), channel_id=1, source_target_pairs={{0,2},{2,0},{1,3},{3,1},{4,6},{6,4},{5,7},{7,5},{8,10},{10,8},{9,1... | collective-permute-start | bytes 1572872 | tf_op jit(solution)/shard_map/ppermute | solution.py:14
  41.3 23.5 %collective-permute-done.1 = bf16[64,64,64]{2,1,0:T(8,128)(2,1)S(1)} collective-permute-done((bf16[64,64,64]{2,1,0:T(8,128)(2,1)S(1)}, bf16[64,64,64]{2,1,0:T(8,128)(2,1)S(1)}, u32[]{:S(2)}, u32[]{:S(2)}) %collective-permute-start.1) | collective-permute-done | bytes 524320 | tf_op jit(solution)/shard_map/ppermute | solution.py:14
  64.8 0.7 convolution_convert_fusion.3
  65.5 1.8 %collective-permute-start.2 = (bf16[64,64,64]{2,1,0:T(8,128)(2,1)S(1)}, bf16[64,64,64]{2,1,0:T(8,128)(2,1)S(1)}, u32[]{:S(2)}, u32[]{:S(2)}) collective-permute-start(bf16[64,64,64]{2,1,0:T(8,128)(2,1)S(1)} %convolution_convert_fusion.3), channel_id=1, source_target_pairs={{0,4},{4,0},{8,12},{12,8},{16,20},{20,16},{24,28},{28,24},{1,5},{5... | collective-permute-start | bytes 1572872 | tf_op jit(solution)/shard_map/ppermute | solution.py:14
  67.3 23.0 %collective-permute-done.2 = bf16[64,64,64]{2,1,0:T(8,128)(2,1)S(1)} collective-permute-done((bf16[64,64,64]{2,1,0:T(8,128)(2,1)S(1)}, bf16[64,64,64]{2,1,0:T(8,128)(2,1)S(1)}, u32[]{:S(2)}, u32[]{:S(2)}) %collective-permute-start.2) | collective-permute-done | bytes 524320 | tf_op jit(solution)/shard_map/ppermute | solution.py:14
  90.3 0.0 copy-done.6
  90.3 0.7 convolution_convert_fusion.2
  91.0 1.5 collective-permute-start.3
  92.6 22.3 %collective-permute-done.3 = bf16[64,64,64]{2,1,0:T(8,128)(2,1)S(1)} collective-permute-done((bf16[64,64,64]{2,1,0:T(8,128)(2,1)S(1)}, bf16[64,64,64]{2,1,0:T(8,128)(2,1)S(1)}, u32[]{:S(2)}, u32[]{:S(2)}) %collective-permute-start.3) | collective-permute-done | bytes 524320 | tf_op jit(solution)/shard_map/ppermute | solution.py:14
  114.9 0.7 convolution_convert_fusion.1
  115.6 2.2 %collective-permute-start.4 = (bf16[64,64,64]{2,1,0:T(8,128)(2,1)S(1)}, bf16[64,64,64]{2,1,0:T(8,128)(2,1)}, u32[]{:S(2)}, u32[]{:S(2)}) collective-permute-start(bf16[64,64,64]{2,1,0:T(8,128)(2,1)S(1)} %convolution_convert_fusion.1), channel_id=1, source_target_pairs={{0,16},{16,0},{4,20},{20,4},{8,24},{24,8},{12,28},{28,12},{1,17},{... | collective-permute-start | bytes 1572872 | tf_op jit(solution)/shard_map/ppermute | solution.py:14
  117.8 44.2 %collective-permute-done.4 = bf16[64,64,64]{2,1,0:T(8,128)(2,1)} collective-permute-done((bf16[64,64,64]{2,1,0:T(8,128)(2,1)S(1)}, bf16[64,64,64]{2,1,0:T(8,128)(2,1)}, u32[]{:S(2)}, u32[]{:S(2)}) %collective-permute-start.4) | collective-permute-done | bytes 524320 | tf_op jit(solution)/shard_map/ppermute | solution.py:14
  162.0 0.0 copy-done
  162.0 4.2 %convert_bitcast_fusion = bf16[64,8,8,256]{3,2,1,0:T(8,128)(2,1)} fusion(bf16[64,64,256]{2,1,0:T(8,128)(2,1)S(1)} %copy-done, bf16[64,64,64]{2,1,0:T(8,128)(2,1)} %collective-permute-done.4, bf16[64,64,64]{2,1,0:T(8,128)(2,1)S(1)} %convolution_convert_fusion.1, bf16[64,3,64,128]{3,2,1,0:T(8,128)(2,1)} %param.10), kind=kOutput, calls=%fused_computation.3 | convolution fusion | flops 204734464 | bytes 6815744 | tf_op jit(solution)/shard_map/kvr,krl->vkl/dot_general | solution.py:54
  166.2 3.0 %copy.41 = bf16[64,8,8,256]{3,2,0,1:T(8,128)(2,1)} copy(bf16[64,8,8,256]{3,2,1,0:T(8,128)(2,1)} %convert_bitcast_fusion) | data formatting | bytes 4194304 | tf_op jit(solution)/shard_map/convert_element_type | solution.py:55
Async XLA Ops:
  0.0 162.0 %copy-start = (bf16[64,64,256]{2,1,0:T(8,128)(2,1)S(1)}, bf16[64,64,256]{2,1,0:T(8,128)(2,1)}, u32[]{:S(2)}) copy-start(bf16[64,64,256]{2,1,0:T(8,128)(2,1)} %param.11) | copy-start | bytes 6291460
  7.4 2.4 %copy-start.1 = (bf16[64,64,64]{2,1,0:T(8,128)(2,1)S(1)}, bf16[64,64,64]{2,1,0:T(8,128)(2,1)}, u32[]{:S(2)}) copy-start(bf16[64,64,64]{2,1,0:T(8,128)(2,1)} %convolution_convert_fusion.10) | copy-start | bytes 1572868
  13.1 2.4 %copy-start.2 = (bf16[64,64,64]{2,1,0:T(8,128)(2,1)S(1)}, bf16[64,64,64]{2,1,0:T(8,128)(2,1)}, u32[]{:S(2)}) copy-start(bf16[64,64,64]{2,1,0:T(8,128)(2,1)} %convolution_convert_fusion.9) | copy-start | bytes 1572868
  18.7 2.4 %copy-start.3 = (bf16[64,64,64]{2,1,0:T(8,128)(2,1)S(1)}, bf16[64,64,64]{2,1,0:T(8,128)(2,1)}, u32[]{:S(2)}) copy-start(bf16[64,64,64]{2,1,0:T(8,128)(2,1)} %convolution_convert_fusion.8) | copy-start | bytes 1572868
  24.4 2.4 %copy-start.4 = (bf16[64,64,64]{2,1,0:T(8,128)(2,1)S(1)}, bf16[64,64,64]{2,1,0:T(8,128)(2,1)}, u32[]{:S(2)}) copy-start(bf16[64,64,64]{2,1,0:T(8,128)(2,1)} %convolution_convert_fusion.7) | copy-start | bytes 1572868
  30.0 2.4 %copy-start.5 = (bf16[64,64,64]{2,1,0:T(8,128)(2,1)S(1)}, bf16[64,64,64]{2,1,0:T(8,128)(2,1)}, u32[]{:S(2)}) copy-start(bf16[64,64,64]{2,1,0:T(8,128)(2,1)} %convolution_convert_fusion.6) | copy-start | bytes 1572868
  32.3 5.3 %copy-start.7 = (bf16[64,2,64,128]{3,2,1,0:T(8,128)(2,1)S(1)}, bf16[64,2,64,128]{3,2,1,0:T(8,128)(2,1)}, u32[]{:S(2)}) copy-start(bf16[64,2,64,128]{3,2,1,0:T(8,128)(2,1)} %param.9) | copy-start | bytes 6291460
  34.8 2.8 %collective-permute-start = (bf16[64,64,64]{2,1,0:T(8,128)(2,1)S(1)}, bf16[64,64,64]{2,1,0:T(8,128)(2,1)S(1)}, u32[]{:S(2)}, u32[]{:S(2)}) collective-permute-start(bf16[64,64,64]{2,1,0:T(8,128)(2,1)S(1)} %convolution_convert_fusion.5), channel_id=1, source_target_pairs={{0,1},{1,0},{2,3},{3,2},{4,5},{5,4},{6,7},{7,6},{8,9},{9,8},{10,11... | collective-permute-start | bytes 1572872 | tf_op jit(solution)/shard_map/ppermute | solution.py:14
  38.3 51.9 %copy-start.6 = (bf16[64,3,64,128]{3,2,1,0:T(8,128)(2,1)S(1)}, bf16[64,3,64,128]{3,2,1,0:T(8,128)(2,1)}, u32[]{:S(2)}) copy-start(bf16[64,3,64,128]{3,2,1,0:T(8,128)(2,1)} %param.10) | copy-start | bytes 9437188
  38.4 26.4 %collective-permute-start.1 = (bf16[64,64,64]{2,1,0:T(8,128)(2,1)S(1)}, bf16[64,64,64]{2,1,0:T(8,128)(2,1)S(1)}, u32[]{:S(2)}, u32[]{:S(2)}) collective-permute-start(bf16[64,64,64]{2,1,0:T(8,128)(2,1)S(1)} %convolution_convert_fusion.4), channel_id=1, source_target_pairs={{0,2},{2,0},{1,3},{3,1},{4,6},{6,4},{5,7},{7,5},{8,10},{10,8},{9,1... | collective-permute-start | bytes 1572872 | tf_op jit(solution)/shard_map/ppermute | solution.py:14
  65.5 24.8 %collective-permute-start.2 = (bf16[64,64,64]{2,1,0:T(8,128)(2,1)S(1)}, bf16[64,64,64]{2,1,0:T(8,128)(2,1)S(1)}, u32[]{:S(2)}, u32[]{:S(2)}) collective-permute-start(bf16[64,64,64]{2,1,0:T(8,128)(2,1)S(1)} %convolution_convert_fusion.3), channel_id=1, source_target_pairs={{0,4},{4,0},{8,12},{12,8},{16,20},{20,16},{24,28},{28,24},{1,5},{5... | collective-permute-start | bytes 1572872 | tf_op jit(solution)/shard_map/ppermute | solution.py:14
  91.0 23.9 %collective-permute-start.3 = (bf16[64,64,64]{2,1,0:T(8,128)(2,1)S(1)}, bf16[64,64,64]{2,1,0:T(8,128)(2,1)S(1)}, u32[]{:S(2)}, u32[]{:S(2)}) collective-permute-start(bf16[64,64,64]{2,1,0:T(8,128)(2,1)S(1)} %convolution_convert_fusion.2), channel_id=1, source_target_pairs={{0,8},{8,0},{4,12},{12,4},{16,24},{24,16},{20,28},{28,20},{1,9},{9... | collective-permute-start | bytes 1572872 | tf_op jit(solution)/shard_map/ppermute | solution.py:14
  115.6 46.4 %collective-permute-start.4 = (bf16[64,64,64]{2,1,0:T(8,128)(2,1)S(1)}, bf16[64,64,64]{2,1,0:T(8,128)(2,1)}, u32[]{:S(2)}, u32[]{:S(2)}) collective-permute-start(bf16[64,64,64]{2,1,0:T(8,128)(2,1)S(1)} %convolution_convert_fusion.1), channel_id=1, source_target_pairs={{0,16},{16,0},{4,20},{20,4},{8,24},{24,8},{12,28},{28,12},{1,17},{... | collective-permute-start | bytes 1572872 | tf_op jit(solution)/shard_map/ppermute | solution.py:14
where the time goes:
time: 170 us; the launch traced here: 169 us
  waiting for transfers between devices  115 us (68%)
  matrix products  29 us (17%)
  local copies, waits for them, and re-layouts  16 us (9%)
  starting transfers between devices  8.98 us (5%)
    ppermute x5, waiting for transfers between devices, swapped(): return lax.ppermute(block, axis, route)  115 us
    dot_general x10, matrix products, mix_level(): jnp.einsum('kvs,kqs->kvq', joined, factors, preferred_element_type=jnp.fl...  21.7 us
    rev x6, local copies, waits for them, and re-layouts, flip_blocks(): return lax.rev(grouped, (block_dim + 1,)).reshape(shape_now)  12.9 us
    ppermute x5, starting transfers between devices, swapped(): return lax.ppermute(block, axis, route)  8.98 us
    dot_general x1, matrix products, body(): jnp.einsum('kvr,krl->vkl', current, leaf_out, preferred_element_type=jnp....  4.17 us
  transfers between devices with their start and end apart: 5, of which 5 were waited for; matrix products, arithmetic and copies ran while one was open for 0% of the time, Pallas kernels for 0%

commit v1 on v0

v1 whole, which is shorter than its diff:
```python
import functools

import jax
import jax.numpy as jnp
from jax import lax
from jax.experimental import pallas as pl
from jax.experimental.pallas import tpu as pltpu
from jax.sharding import PartitionSpec as P

NT = (((1,), (1,)), ((), ()))
PIECES = 4
SHARES = (5, 9, 10, 8)
LAGS = (
    (1.0, 1.1, 1.2, 1.3),
    (0.0, 0.5, 1.2, 1.6),
    (0.0, 0.5, 1.1, 1.6),
    (0.0, 0.5, 1.2, 2.15),
    (0.0, 0.9, 1.1, 2.1),
)


def half_swap(x):
    half = x.shape[1] // 2
    return jnp.concatenate([x[:, half:], x[:, :half]], axis=1)


def pack(product):
    rows = product.shape[0] // 2
    top, bottom = product[:rows], product[rows:]
    low = lax.broadcasted_iota(jnp.int32, top.shape, 1) < top.shape[1] // 2
    return jnp.where(low, top, bottom)


def mix_pair(own, other, factors):
    joined = jnp.concatenate([own, other], axis=0)
    rows, width = factors.shape[1:]
    product = jnp.dot(
        factors.reshape(2 * rows, width), joined, preferred_element_type=jnp.float32
    )
    return pack(product)


def local_kernel(
    src_hbm,
    leaf_hbm,
    mix_hbm,
    lo_hbm,
    first,
    state,
    last_mix,
    lo_mix,
    even,
    odd,
    src,
    leaf,
    mix,
    src_sem,
    leaf_sem,
    mix_sem,
    lo_sem,
):
    pairs = even.shape[0]
    blocks = leaf.shape[0]
    levels = mix_hbm.shape[1]
    width = leaf.shape[2]

    def inputs(piece):
        count = blocks // PIECES
        cols = pl.ds(piece * count * width, count * width)
        rows = pl.ds(piece * count, count)
        return (
            pltpu.make_async_copy(src_hbm.at[:, cols], src.at[:, cols], src_sem.at[piece]),
            pltpu.make_async_copy(leaf_hbm.at[rows], leaf.at[rows], leaf_sem.at[piece]),
        )

    def factors(level):
        held = mix.at[level] if level < levels - 1 else last_mix
        return pltpu.make_async_copy(mix_hbm.at[:, level], held, mix_sem.at[level])

    next_levels = pltpu.make_async_copy(lo_hbm, lo_mix, lo_sem)
    for piece in range(PIECES):
        for copy in inputs(piece):
            copy.start()

    queue = [factors(level) for level in range(levels)]
    for piece in range(PIECES):
        for copy in inputs(piece):
            copy.wait()
        for copy in queue[piece * levels // PIECES : (piece + 1) * levels // PIECES]:
            copy.start()
        for pair in range(piece * pairs // PIECES, (piece + 1) * pairs // PIECES):
            columns = [src[:, pl.ds((2 * pair + side) * width, width)] for side in range(2)]
            product = lax.dot_general(
                leaf[2 * pair : 2 * pair + 2].reshape(-1, width),
                jnp.concatenate(columns, axis=0),
                NT,
                preferred_element_type=jnp.float32,
            )
            even[pair] = pack(product).astype(even.dtype)
    next_levels.start()

    for level in range(levels):
        factors(level).wait()
        old, new = (odd, even) if level % 2 else (even, odd)
        if level == levels - 2:
            new = state
        if level == levels - 1:
            old, new = state, first
        for pair in range(new.shape[0]):
            own = old[pair]
            other = half_swap(own) if level == 0 else old[pair ^ 1 << level - 1]
            chosen = last_mix if level == levels - 1 else mix.at[level]
            part = chosen[2 * pair : 2 * pair + 2]
            new[pair] = mix_pair(own, other, part).astype(own.dtype)
    next_levels.wait()


def local_phase(sources, leaf_in, local_mix, lo_mix, size):
    vectors = sources.shape[0]
    blocks, rank, _ = leaf_in.shape
    levels = local_mix.shape[1]
    return pl.pallas_call(
        local_kernel,
        out_shape=[
            pltpu.VMEM((size, rank, 2 * vectors), jnp.bfloat16),
            pltpu.VMEM((blocks // 2, rank, 2 * vectors), jnp.bfloat16),
            pltpu.VMEM((blocks,) + local_mix.shape[2:], local_mix.dtype),
            pltpu.VMEM(lo_mix.shape, lo_mix.dtype),
        ],
        in_specs=[pl.BlockSpec(memory_space=pltpu.HBM)] * 4,
        out_specs=[pl.BlockSpec(memory_space=pltpu.VMEM)] * 4,
        scratch_shapes=[
            pltpu.VMEM((blocks // 2, rank, 2 * vectors), jnp.bfloat16),
            pltpu.VMEM((blocks // 2, rank, 2 * vectors), jnp.bfloat16),
            pltpu.VMEM(sources.shape, sources.dtype),
            pltpu.VMEM(leaf_in.shape, leaf_in.dtype),
            pltpu.VMEM((levels - 1, blocks) + local_mix.shape[2:], local_mix.dtype),
            pltpu.SemaphoreType.DMA((PIECES,)),
            pltpu.SemaphoreType.DMA((PIECES,)),
            pltpu.SemaphoreType.DMA((levels,)),
            pltpu.SemaphoreType.DMA,
        ],
        compiler_params=pltpu.CompilerParams(vmem_limit_bytes=58 << 20),
        cost_estimate=pl.CostEstimate(flops=10**9, bytes_accessed=10 << 20, transcendentals=0),
        name="local_levels",
    )(sources, leaf_in, local_mix, lo_mix)


def rest_kernel(start, state_ref, mix_ref, after_ref, out_ref):
    pairs = state_ref.shape[0]
    for p in range(out_ref.shape[0]):
        pair = start + p
        other = state_ref[pair ^ pairs // 2]
        mixed = mix_pair(state_ref[pair], other, mix_ref[2 * pair : 2 * pair + 2])
        out_ref[p] = mixed.astype(out_ref.dtype)


def local_rest(state, last_mix, start, stop, after):
    _, rank, lanes = state.shape
    return pl.pallas_call(
        functools.partial(rest_kernel, start),
        out_shape=pltpu.VMEM((stop - start, rank, lanes), state.dtype),
        in_specs=[pl.BlockSpec(memory_space=pltpu.VMEM)] * 2 + [pl.BlockSpec(memory_space=pl.ANY)],
        out_specs=pl.BlockSpec(memory_space=pltpu.VMEM),
        compiler_params=pltpu.CompilerParams(vmem_limit_bytes=8 << 20),
        cost_estimate=pl.CostEstimate(flops=3 * 10**9, bytes_accessed=0, transcendentals=0),
        name="local_rest",
    )(state, last_mix, after)


def cross_kernel(level, start, offset, own_ref, other_ref, mix_ref, after_ref, out_ref):
    for p in range(out_ref.shape[0]):
        block = 2 * (start + p)
        mixed = mix_pair(
            own_ref[offset + p], other_ref[offset + p], mix_ref[block : block + 2, level]
        )
        out_ref[p] = mixed.astype(out_ref.dtype)


def cross_level(own, other, mix, level, start, offset, size, after):
    _, rank, lanes = own.shape
    return pl.pallas_call(
        functools.partial(cross_kernel, level, start, offset),
        out_shape=pltpu.VMEM((size, rank, lanes), own.dtype),
        in_specs=[pl.BlockSpec(memory_space=pltpu.VMEM)] * 3 + [pl.BlockSpec(memory_space=pl.ANY)],
        out_specs=pl.BlockSpec(memory_space=pltpu.VMEM),
        compiler_params=pltpu.CompilerParams(vmem_limit_bytes=8 << 20),
        cost_estimate=pl.CostEstimate(flops=3 * 10**9, bytes_accessed=0, transcendentals=0),
        name="cross_level",
    )(own, other, mix, after)


def final_kernel(has_token, level, start, own_ref, other_ref, mix_ref, leaf_ref, *rest):
    out_hbm, *tokens, held, sem = rest[-4 if has_token else -3 :]
    for token in tokens:
        token[...] = jnp.zeros_like(token)
    pairs = own_ref.shape[0]
    vectors = held.shape[0]
    width = leaf_ref.shape[2]
    turned = []
    for p in range(pairs):
        block = 2 * (start + p)
        mixed = mix_pair(own_ref[p], other_ref[p], mix_ref[block : block + 2, level])
        turned.append(mixed.astype(jnp.bfloat16).T)
    copies = []
    for first, stop in ((0, pairs // 2), (pairs // 2, pairs)):
        for p in range(first, stop):
            for side in range(2):
                held[:, pl.ds((2 * p + side) * width, width)] = jnp.dot(
                    turned[p][side * vectors : (side + 1) * vectors],
                    leaf_ref[2 * (start + p) + side],
                    preferred_element_type=jnp.float32,
                ).astype(held.dtype)
        count = 2 * (stop - first) * width
        copies.append(
            pltpu.make_async_copy(
                held.at[:, pl.ds(2 * first * width, count)],
                out_hbm.at[:, pl.ds(2 * (start + first) * width, count)],
                sem.at[len(copies)],
            )
        )
        copies[-1].start()
    for copy in copies:
        copy.wait()


def final_level(own, other, mix, leaf_out, level, start, so_far, after, has_token):
    blocks, rank, width = leaf_out.shape
    pairs, _, lanes = own.shape
    vectors = lanes // 2
    in_specs = [pl.BlockSpec(memory_space=pltpu.VMEM)] * 4 + [pl.BlockSpec(memory_space=pl.ANY)]
    operands = [own, other, mix, leaf_out, after]
    aliases = {}
    if so_far is not None:
        in_specs.append(pl.BlockSpec(memory_space=pltpu.HBM))
        operands.append(so_far)
        aliases = {5: 0}
    return pl.pallas_call(
        functools.partial(final_kernel, has_token, level, start),
        out_shape=[jax.ShapeDtypeStruct((vectors, blocks * width), own.dtype)]
        + [pltpu.VMEM((8, lanes), jnp.float32)] * has_token,
        in_specs=in_specs,
        out_specs=[pl.BlockSpec(memory_space=pltpu.HBM)]
        + [pl.BlockSpec(memory_space=pltpu.VMEM)] * has_token,
        scratch_shapes=[
            pltpu.VMEM((vectors, 2 * pairs * width), own.dtype),
            pltpu.SemaphoreType.DMA((2,)),
        ],
        input_output_aliases=aliases,
        compiler_params=pltpu.CompilerParams(vmem_limit_bytes=8 << 20),
        cost_estimate=pl.CostEstimate(flops=3 * 10**9, bytes_accessed=0, transcendentals=0),
        name="final_level",
    )(*operands)


def swapped(block, axis, stride):
    count = lax.axis_size(axis)
    route = [(i, i ^ (1 << stride)) for i in range(count)]
    return lax.ppermute(block, axis, route)


def cut(total, shares):
    ends = [total * sum(shares[: c + 1]) // sum(shares) for c in range(len(shares))]
    return list(zip([0] + ends[:-1], ends))


def body(sources, leaf_in, local_mix, lo_mix, hi_mix, leaf_out):
    lo_levels = lax.axis_size("lo").bit_length() - 1
    hi_levels = lax.axis_size("hi").bit_length() - 1
    pairs = leaf_in.shape[0] // 2
    steps = [("lo", n, lo_mix) for n in range(lo_levels)]
    steps += [("hi", n, hi_mix) for n in range(hi_levels)]
    end = len(steps) - 1
    parts = cut(pairs, SHARES)
    head = parts[0][1]
    waiting = {}

    def turn(item):
        s, c = item
        lags = LAGS[min(end - s, 3) if s else 4]
        return s + lags[c], -s

    first, state, last_mix, lo_mix = local_phase(sources, leaf_in, local_mix, lo_mix, head)
    steps[:lo_levels] = [("lo", n, lo_mix) for n in range(lo_levels)]
    axis, level, _ = steps[0]
    waiting[0, 0] = first, swapped(first, axis, level), 0
    after = state
    targets = None
    for s, c in sorted(((s, c) for s in range(end + 1) for c in range(len(parts))), key=turn):
        own, other, offset = waiting.pop((s, c))
        _, level, mix = steps[s]
        start, stop = parts[c]
        if s == end:
            more = c < len(parts) - 1
            targets, *tokens = final_level(
                own, other, mix, leaf_out, level, start, targets, after, more
            )
            after = tokens[0] if more else None
            continue
        block = after = cross_level(own, other, mix, level, start, offset, stop - start, after)
        if s == 0 and c == 0:
            after = local_rest(state, last_mix, *parts[1], after)
            waiting[0, 1] = after, swapped(after, *steps[0][:2]), 0
        if s == 0 and c == 1:
            after = rest = local_rest(state, last_mix, stop, pairs, after)
            partner = swapped(rest, *steps[0][:2])
            for d in range(2, len(parts)):
                waiting[0, d] = rest, partner, parts[d][0] - stop
        axis, level, _ = steps[s + 1]
        waiting[s + 1, c] = block, swapped(block, axis, level), 0
    return targets


def solution(mesh):
    return jax.shard_map(
        body,
        mesh=mesh,
        in_specs=(
            P(None, ("hi", "lo")),
            P(("hi", "lo"), None, None),
            P(("hi", "lo"), None, None, None),
            P(("hi", "lo"), None, None, None),
            P(("hi", "lo"), None, None, None),
            P(("hi", "lo"), None, None),
        ),
        out_specs=P(None, ("hi", "lo")),
        check_vma=False,
    )
```

time: 170 us -> 53.7 us (0.32)
  waiting for transfers between devices: 115 us -> 12.2 us
  matrix products: 29 us -> 0 us
  starting transfers between devices: 8.98 us -> 26.7 us
  local copies, waits for them, and re-layouts: 16 us -> 0.01 us
  Pallas kernels: 0 us -> 14.3 us
    ppermute x5 -> x19, waiting for transfers between devices: 115 us -> 12.2 us  [swapped(): return lax.ppermute(block, axis, route)]
    dot_general x12 -> x0, matrix products: 29 us -> none  [the longest x10 21.7 us: mix_level(): jnp.einsum('kvs,kqs->kvq', joined, factors, preferred_element_type=jnp.fl...]
    ppermute x5 -> x19, starting transfers between devices: 8.98 us -> 26.7 us  [swapped(): return lax.ppermute(block, axis, route)]
    pallas_call x0 -> x23, Pallas kernels: none -> 14.3 us  [the longest x1 5.25 us: local_phase(): pl.pallas_call(local_kernel, out_shape=[pltpu.VMEM((size, rank, 2 * vecto...]
    rev x6 -> x0, local copies, waits for them, and re-layouts: 12.9 us -> none  [flip_blocks(): return lax.rev(grouped, (block_dim + 1,)).reshape(shape_now)]
    convert_element_type x1 -> x0, local copies, waits for them, and re-layouts: 3.04 us -> none  [body(): return result.reshape(vectors, blocks_here * leaf_size).astype(jnp.bfloat16)]
  transfers between devices with their start and end apart: 5 -> 19, of which waited for: 5 -> 10; matrix products, arithmetic and copies ran while one was open for 0% -> 0% of each run, Pallas kernels for 0% -> 14%
where the time goes in v1:
time: 53.7 us; the launch traced here: 53.5 us
  starting transfers between devices  26.7 us (50%)
  Pallas kernels  14.3 us (27%)
  waiting for transfers between devices  12.2 us (23%)
    ppermute x19, starting transfers between devices, swapped(): return lax.ppermute(block, axis, route)  26.7 us
    ppermute x19, waiting for transfers between devices, swapped(): return lax.ppermute(block, axis, route)  12.2 us
    pallas_call x1, Pallas kernels, local_phase(): pl.pallas_call(local_kernel, out_shape=[pltpu.VMEM((size, rank, 2 * vecto...  5.25 us
    pallas_call x4, Pallas kernels, final_level(): pl.pallas_call(functools.partial(final_kernel, has_token, level, start),...  5 us
    pallas_call x16, Pallas kernels, cross_level(): pl.pallas_call(functools.partial(cross_kernel, level, start, offset), out...  3.55 us
  transfers between devices with their start and end apart: 19, of which 10 were waited for; matrix products, arithmetic and copies ran while one was open for 0% of the time, Pallas kernels for 14%

profile of v1, /device:TPU:0, one launch (start us, length us, event | category | flops | bytes accessed | tf_op | source)
XLA Modules:
  0.0 53.5 jit_solution(2235867623652530813)
XLA Ops:
  0.0 5.3 %local_levels.1 = (bf16[5,64,128]{2,1,0:T(8,128)(2,1)S(1)}, bf16[32,64,128]{2,1,0:T(8,128)(2,1)S(1)}, bf16[64,64,128]{2,1,0:T(8,128)(2,1)S(1)}, bf16[64,2,64,128]{3,2,1,0:T(8,128)(2,1)S(1)}) custom-call(bf16[64,16384]{1,0:T(8,128)(2,1)} %src_hbm.1, bf16[64,64,256]{2,1,0:T(8,128)(2,1)} %leaf_hbm.1, bf16[64,6,64,128]{3,2,1,0:T(8,128)(2,1)} %mix_hbm.1, ...), custom_call_target="tpu_custom_call" | custom-call | flops 1000000000 | bytes 10485760 | tf_op jit(solution)/shard_map/local_levels/pallas_call | solution.py:122
  5.3 0.5 collective-permute-start
  5.8 0.9 %collective-permute-done.other_ref = bf16[5,64,128]{2,1,0:T(8,128)(2,1)S(1)} collective-permute-done((bf16[5,64,128]{2,1,0:T(8,128)(2,1)S(1)}, bf16[5,64,128]{2,1,0:T(8,128)(2,1)S(1)}, u32[]{:S(2)}, u32[]{:S(2)}) %collective-permute-start) | collective-permute-done | bytes 81952 | tf_op jit(solution)/shard_map/ppermute | solution.py:259
  6.9 0.2 local_rest.2.own_ref.after_ref
  7.1 0.4 collective-permute-start.1
  7.6 2.7 %collective-permute-start.3 = (bf16[5,64,128]{2,1,0:T(8,128)(2,1)S(1)}, bf16[5,64,128]{2,1,0:T(8,128)(2,1)S(1)}, u32[]{:S(2)}, u32[]{:S(2)}) collective-permute-start(bf16[5,64,128]{2,1,0:T(8,128)(2,1)S(1)} %cross_level.16.after_ref.own_ref), channel_id=1, source_target_pairs={{0,2},{1,3},{2,0},{3,1},{4,6},{5,7},{6,4},{7,5},{8,10},{9,11},{10,... | collective-permute-start | bytes 245768 | tf_op jit(solution)/shard_map/ppermute | solution.py:259
  10.2 0.2 cross_level.17.after_ref.own_ref
  10.5 0.3 local_rest.3.after_ref.own_ref
  10.9 1.3 %collective-permute-start.5 = (bf16[9,64,128]{2,1,0:T(8,128)(2,1)S(1)}, bf16[9,64,128]{2,1,0:T(8,128)(2,1)S(1)}, u32[]{:S(2)}, u32[]{:S(2)}) collective-permute-start(bf16[9,64,128]{2,1,0:T(8,128)(2,1)S(1)} %cross_level.17.after_ref.own_ref), channel_id=1, source_target_pairs={{0,2},{1,3},{2,0},{3,1},{4,6},{5,7},{6,4},{7,5},{8,10},{9,11},{10,... | collective-permute-start | bytes 442376 | tf_op jit(solution)/shard_map/ppermute | solution.py:259
  12.2 1.0 %collective-permute-done.3.other_ref = bf16[5,64,128]{2,1,0:T(8,128)(2,1)S(1)} collective-permute-done((bf16[5,64,128]{2,1,0:T(8,128)(2,1)S(1)}, bf16[5,64,128]{2,1,0:T(8,128)(2,1)S(1)}, u32[]{:S(2)}, u32[]{:S(2)}) %collective-permute-start.3) | collective-permute-done | bytes 81952 | tf_op jit(solution)/shard_map/ppermute | solution.py:259
  13.2 0.2 cross_level.18.after_ref.own_ref
  13.4 1.8 %collective-permute-start.4 = (bf16[5,64,128]{2,1,0:T(8,128)(2,1)S(1)}, bf16[5,64,128]{2,1,0:T(8,128)(2,1)S(1)}, u32[]{:S(2)}, u32[]{:S(2)}) collective-permute-start(bf16[5,64,128]{2,1,0:T(8,128)(2,1)S(1)} %cross_level.18.after_ref.own_ref), channel_id=1, source_target_pairs={{0,4},{4,0},{8,12},{12,8},{16,20},{20,16},{24,28},{28,24},{1,5},{5... | collective-permute-start | bytes 245768 | tf_op jit(solution)/shard_map/ppermute | solution.py:259
  15.2 0.2 cross_level.19.after_ref.own_ref
  15.4 1.6 %collective-permute-start.7 = (bf16[10,64,128]{2,1,0:T(8,128)(2,1)S(1)}, bf16[10,64,128]{2,1,0:T(8,128)(2,1)S(1)}, u32[]{:S(2)}, u32[]{:S(2)}) collective-permute-start(bf16[10,64,128]{2,1,0:T(8,128)(2,1)S(1)} %cross_level.19.after_ref.own_ref), channel_id=1, source_target_pairs={{0,2},{1,3},{2,0},{3,1},{4,6},{5,7},{6,4},{7,5},{8,10},{9,11},{10,... | collective-permute-start | bytes 491528 | tf_op jit(solution)/shard_map/ppermute | solution.py:259
  17.1 0.2 cross_level.20.after_ref.own_ref
  17.4 2.0 %collective-permute-start.10 = (bf16[9,64,128]{2,1,0:T(8,128)(2,1)S(1)}, bf16[9,64,128]{2,1,0:T(8,128)(2,1)S(1)}, u32[]{:S(2)}, u32[]{:S(2)}) collective-permute-start(bf16[9,64,128]{2,1,0:T(8,128)(2,1)S(1)} %cross_level.20.after_ref.own_ref), channel_id=1, source_target_pairs={{0,4},{4,0},{8,12},{12,8},{16,20},{20,16},{24,28},{28,24},{1,5},{5... | collective-permute-start | bytes 442376 | tf_op jit(solution)/shard_map/ppermute | solution.py:259
  19.4 0.2 cross_level.21.after_ref.own_ref
  19.6 1.6 %collective-permute-start.9 = (bf16[5,64,128]{2,1,0:T(8,128)(2,1)S(1)}, bf16[5,64,128]{2,1,0:T(8,128)(2,1)S(1)}, u32[]{:S(2)}, u32[]{:S(2)}) collective-permute-start(bf16[5,64,128]{2,1,0:T(8,128)(2,1)S(1)} %cross_level.21.after_ref.own_ref), channel_id=1, source_target_pairs={{0,8},{4,12},{8,0},{12,4},{16,24},{20,28},{24,16},{28,20},{1,9},{5... | collective-permute-start | bytes 245768 | tf_op jit(solution)/shard_map/ppermute | solution.py:259
  21.2 0.2 cross_level.22.after_ref.own_ref
  21.4 1.2 %collective-permute-start.6 = (bf16[8,64,128]{2,1,0:T(8,128)(2,1)S(1)}, bf16[8,64,128]{2,1,0:T(8,128)(2,1)S(1)}, u32[]{:S(2)}, u32[]{:S(2)}) collective-permute-start(bf16[8,64,128]{2,1,0:T(8,128)(2,1)S(1)} %cross_level.22.after_ref.own_ref), channel_id=1, source_target_pairs={{0,2},{1,3},{2,0},{3,1},{4,6},{5,7},{6,4},{7,5},{8,10},{9,11},{10,... | collective-permute-start | bytes 393224 | tf_op jit(solution)/shard_map/ppermute | solution.py:259
  22.6 0.2 cross_level.23.after_ref.own_ref
  22.8 0.7 %collective-permute-start.8 = (bf16[10,64,128]{2,1,0:T(8,128)(2,1)S(1)}, bf16[10,64,128]{2,1,0:T(8,128)(2,1)S(1)}, u32[]{:S(2)}, u32[]{:S(2)}) collective-permute-start(bf16[10,64,128]{2,1,0:T(8,128)(2,1)S(1)} %cross_level.23.after_ref.own_ref), channel_id=1, source_target_pairs={{0,4},{4,0},{8,12},{12,8},{16,20},{20,16},{24,28},{28,24},{1,5},{5... | collective-permute-start | bytes 491528 | tf_op jit(solution)/shard_map/ppermute | solution.py:259
  23.6 0.2 cross_level.24.after_ref.own_ref
  23.8 0.9 %collective-permute-start.12 = (bf16[9,64,128]{2,1,0:T(8,128)(2,1)S(1)}, bf16[9,64,128]{2,1,0:T(8,128)(2,1)S(1)}, u32[]{:S(2)}, u32[]{:S(2)}) collective-permute-start(bf16[9,64,128]{2,1,0:T(8,128)(2,1)S(1)} %cross_level.24.after_ref.own_ref), channel_id=1, source_target_pairs={{0,8},{4,12},{8,0},{12,4},{16,24},{20,28},{24,16},{28,20},{1,9},{5... | collective-permute-start | bytes 442376 | tf_op jit(solution)/shard_map/ppermute | solution.py:259
  24.8 0.2 cross_level.25.after_ref.own_ref
  25.0 2.7 %collective-permute-start.18 = (bf16[5,64,128]{2,1,0:T(8,128)(2,1)S(1)}, bf16[5,64,128]{2,1,0:T(8,128)(2,1)S(1)}, u32[]{:S(2)}, u32[]{:S(2)}) collective-permute-start(bf16[5,64,128]{2,1,0:T(8,128)(2,1)S(1)} %cross_level.25.after_ref.own_ref), channel_id=1, source_target_pairs={{0,16},{4,20},{8,24},{12,28},{16,0},{20,4},{24,8},{28,12},{1,17},{... | collective-permute-start | bytes 245768 | tf_op jit(solution)/shard_map/ppermute | solution.py:259
  27.6 0.6 %collective-permute-done.8.other_ref = bf16[10,64,128]{2,1,0:T(8,128)(2,1)S(1)} collective-permute-done((bf16[10,64,128]{2,1,0:T(8,128)(2,1)S(1)}, bf16[10,64,128]{2,1,0:T(8,128)(2,1)S(1)}, u32[]{:S(2)}, u32[]{:S(2)}) %collective-permute-start.8) | collective-permute-done | bytes 163872 | tf_op jit(solution)/shard_map/ppermute | solution.py:259
  28.2 0.2 cross_level.26.after_ref.own_ref
  28.5 0.6 %collective-permute-start.14 = (bf16[10,64,128]{2,1,0:T(8,128)(2,1)S(1)}, bf16[10,64,128]{2,1,0:T(8,128)(2,1)S(1)}, u32[]{:S(2)}, u32[]{:S(2)}) collective-permute-start(bf16[10,64,128]{2,1,0:T(8,128)(2,1)S(1)} %cross_level.26.after_ref.own_ref), channel_id=1, source_target_pairs={{0,8},{4,12},{8,0},{12,4},{16,24},{20,28},{24,16},{28,20},{1,9},{5... | collective-permute-start | bytes 491528 | tf_op jit(solution)/shard_map/ppermute | solution.py:259
  29.1 0.2 cross_level.27.after_ref.own_ref
  29.3 1.4 %collective-permute-start.11 = (bf16[8,64,128]{2,1,0:T(8,128)(2,1)S(1)}, bf16[8,64,128]{2,1,0:T(8,128)(2,1)S(1)}, u32[]{:S(2)}, u32[]{:S(2)}) collective-permute-start(bf16[8,64,128]{2,1,0:T(8,128)(2,1)S(1)} %cross_level.27.after_ref.own_ref), channel_id=1, source_target_pairs={{0,4},{4,0},{8,12},{12,8},{16,20},{20,16},{24,28},{28,24},{1,5},{5... | collective-permute-start | bytes 393224 | tf_op jit(solution)/shard_map/ppermute | solution.py:259
  30.8 0.2 collective-permute-done.12.other_ref
  31.0 0.2 cross_level.28.after_ref.own_ref
  31.2 1.9 %collective-permute-start.17 = (bf16[9,64,128]{2,1,0:T(8,128)(2,1)S(1)}, bf16[9,64,128]{2,1,0:T(8,128)(2,1)S(1)}, u32[]{:S(2)}, u32[]{:S(2)}) collective-permute-start(bf16[9,64,128]{2,1,0:T(8,128)(2,1)S(1)} %cross_level.28.after_ref.own_ref), channel_id=1, source_target_pairs={{0,16},{4,20},{8,24},{12,28},{16,0},{20,4},{24,8},{28,12},{1,17},{... | collective-permute-start | bytes 442376 | tf_op jit(solution)/shard_map/ppermute | solution.py:259
  33.1 1.2 %collective-permute-done.11.other_ref = bf16[8,64,128]{2,1,0:T(8,128)(2,1)S(1)} collective-permute-done((bf16[8,64,128]{2,1,0:T(8,128)(2,1)S(1)}, bf16[8,64,128]{2,1,0:T(8,128)(2,1)S(1)}, u32[]{:S(2)}, u32[]{:S(2)}) %collective-permute-start.11) | collective-permute-done | bytes 131104 | tf_op jit(solution)/shard_map/ppermute | solution.py:259
  34.3 0.2 cross_level.29.after_ref.own_ref
  34.6 1.6 %collective-permute-start.13 = (bf16[8,64,128]{2,1,0:T(8,128)(2,1)S(1)}, bf16[8,64,128]{2,1,0:T(8,128)(2,1)S(1)}, u32[]{:S(2)}, u32[]{:S(2)}) collective-permute-start(bf16[8,64,128]{2,1,0:T(8,128)(2,1)S(1)} %cross_level.29.after_ref.own_ref), channel_id=1, source_target_pairs={{0,8},{4,12},{8,0},{12,4},{16,24},{20,28},{24,16},{28,20},{1,9},{5... | collective-permute-start | bytes 393224 | tf_op jit(solution)/shard_map/ppermute | solution.py:259
  36.1 2.4 %collective-permute-done.14.other_ref = bf16[10,64,128]{2,1,0:T(8,128)(2,1)S(1)} collective-permute-done((bf16[10,64,128]{2,1,0:T(8,128)(2,1)S(1)}, bf16[10,64,128]{2,1,0:T(8,128)(2,1)S(1)}, u32[]{:S(2)}, u32[]{:S(2)}) %collective-permute-start.14) | collective-permute-done | bytes 163872 | tf_op jit(solution)/shard_map/ppermute | solution.py:259
  38.5 0.2 cross_level.30.after_ref.own_ref
  38.8 0.3 collective-permute-start.16
  39.1 1.6 %collective-permute-done.13.other_ref = bf16[8,64,128]{2,1,0:T(8,128)(2,1)S(1)} collective-permute-done((bf16[8,64,128]{2,1,0:T(8,128)(2,1)S(1)}, bf16[8,64,128]{2,1,0:T(8,128)(2,1)S(1)}, u32[]{:S(2)}, u32[]{:S(2)}) %collective-permute-start.13) | collective-permute-done | bytes 131104 | tf_op jit(solution)/shard_map/ppermute | solution.py:259
  40.6 0.2 cross_level.31.rest_0_.own_ref
  40.9 3.4 %collective-permute-start.15 = (bf16[8,64,128]{2,1,0:T(8,128)(2,1)S(1)}, bf16[8,64,128]{2,1,0:T(8,128)(2,1)S(1)}, u32[]{:S(2)}, u32[]{:S(2)}) collective-permute-start(bf16[8,64,128]{2,1,0:T(8,128)(2,1)S(1)} %cross_level.31.rest_0_.own_ref), channel_id=1, source_target_pairs={{0,16},{4,20},{8,24},{12,28},{16,0},{20,4},{24,8},{28,12},{1,17},{... | collective-permute-start | bytes 393224 | tf_op jit(solution)/shard_map/ppermute | solution.py:259
  44.3 1.1 %final_level.4 = (bf16[64,16384]{1,0:T(8,128)(2,1)}, f32[8,128]{1,0:T(8,128)S(1)}) custom-call(bf16[5,64,128]{2,1,0:T(8,128)(2,1)S(1)} %cross_level.25.after_ref.own_ref, bf16[5,64,128]{2,1,0:T(8,128)(2,1)S(1)} %collective-permute-done.18.other_ref, bf16[64,3,64,128]{3,2,1,0:T(8,128)(2,1)S(1)} %copy-done, bf16[64,64,256]{2,1,0:T(8,128)(2,1)S(1)} %copy-done.1, ...), custom_call_target="tpu_custom_call" | custom-call | flops 3000000000 | tf_op jit(solution)/shard_map/final_level/pallas_call | solution.py:238
  45.5 1.3 %final_level.5 = (bf16[64,16384]{1,0:T(8,128)(2,1)}, f32[8,128]{1,0:T(8,128)S(1)}) custom-call(bf16[9,64,128]{2,1,0:T(8,128)(2,1)S(1)} %cross_level.28.after_ref.own_ref, bf16[9,64,128]{2,1,0:T(8,128)(2,1)S(1)} %collective-permute-done.17.other_ref, bf16[64,3,64,128]{3,2,1,0:T(8,128)(2,1)S(1)} %copy-done, ...), custom_call_target="tpu_custom_call", output_to_operand_aliasing={{0}: (5, {})} | custom-call | flops 3000000000 | tf_op jit(solution)/shard_map/final_level/pallas_call | solution.py:238
  46.8 4.1 %collective-permute-done.16.other_ref = bf16[10,64,128]{2,1,0:T(8,128)(2,1)S(1)} collective-permute-done((bf16[10,64,128]{2,1,0:T(8,128)(2,1)S(1)}, bf16[10,64,128]{2,1,0:T(8,128)(2,1)S(1)}, u32[]{:S(2)}, u32[]{:S(2)}) %collective-permute-start.16) | collective-permute-done | bytes 163872 | tf_op jit(solution)/shard_map/ppermute | solution.py:259
  50.9 1.3 %final_level.6 = (bf16[64,16384]{1,0:T(8,128)(2,1)}, f32[8,128]{1,0:T(8,128)S(1)}) custom-call(bf16[10,64,128]{2,1,0:T(8,128)(2,1)S(1)} %cross_level.30.after_ref.own_ref, bf16[10,64,128]{2,1,0:T(8,128)(2,1)S(1)} %collective-permute-done.16.other_ref, bf16[64,3,64,128]{3,2,1,0:T(8,128)(2,1)S(1)} %copy-done, ...), custom_call_target="tpu_custom_call", output_to_operand_aliasing={{0}: (5, {})} | custom-call | flops 3000000000 | tf_op jit(solution)/shard_map/final_level/pallas_call | solution.py:238
  52.3 1.3 %final_level.7 = bf16[64,16384]{1,0:T(8,128)(2,1)} custom-call(bf16[8,64,128]{2,1,0:T(8,128)(2,1)S(1)} %cross_level.31.rest_0_.own_ref, bf16[8,64,128]{2,1,0:T(8,128)(2,1)S(1)} %collective-permute-done.15.other_ref, bf16[64,3,64,128]{3,2,1,0:T(8,128)(2,1)S(1)} %copy-done, bf16[64,64,256]{2,1,0:T(8,128)(2,1)S(1)} %copy-done.1, ...), custom_call_target="tpu_custom_call", output_to_operand_aliasing={{}: (5, {})} | custom-call | flops 3000000000 | tf_op jit(solution)/shard_map/final_level/pallas_call | solution.py:238
  (17 shorter events, 0.6 us)
Async XLA Ops:
  5.3 1.4 %collective-permute-start = (bf16[5,64,128]{2,1,0:T(8,128)(2,1)S(1)}, bf16[5,64,128]{2,1,0:T(8,128)(2,1)S(1)}, u32[]{:S(2)}, u32[]{:S(2)}) collective-permute-start(bf16[5,64,128]{2,1,0:T(8,128)(2,1)S(1)} %get-tuple-element.17.own_ref), channel_id=1, source_target_pairs={{0,1},{1,0},{2,3},{3,2},{4,5},{5,4},{6,7},{7,6},{8,9},{9,8},{10,11... | collective-permute-start | bytes 245768 | tf_op jit(solution)/shard_map/ppermute | solution.py:259
  7.1 3.1 %collective-permute-start.1 = (bf16[9,64,128]{2,1,0:T(8,128)(2,1)S(1)}, bf16[9,64,128]{2,1,0:T(8,128)(2,1)S(1)}, u32[]{:S(2)}, u32[]{:S(2)}) collective-permute-start(bf16[9,64,128]{2,1,0:T(8,128)(2,1)S(1)} %local_rest.2.own_ref.after_ref), channel_id=1, source_target_pairs={{0,1},{1,0},{2,3},{3,2},{4,5},{5,4},{6,7},{7,6},{8,9},{9,8},{10,11... | collective-permute-start | bytes 442376 | tf_op jit(solution)/shard_map/ppermute | solution.py:259
  7.6 5.6 %collective-permute-start.3 = (bf16[5,64,128]{2,1,0:T(8,128)(2,1)S(1)}, bf16[5,64,128]{2,1,0:T(8,128)(2,1)S(1)}, u32[]{:S(2)}, u32[]{:S(2)}) collective-permute-start(bf16[5,64,128]{2,1,0:T(8,128)(2,1)S(1)} %cross_level.16.after_ref.own_ref), channel_id=1, source_target_pairs={{0,2},{1,3},{2,0},{3,1},{4,6},{5,7},{6,4},{7,5},{8,10},{9,11},{10,... | collective-permute-start | bytes 245768 | tf_op jit(solution)/shard_map/ppermute | solution.py:259
  10.8 4.4 %collective-permute-start.2 = (bf16[18,64,128]{2,1,0:T(8,128)(2,1)S(1)}, bf16[18,64,128]{2,1,0:T(8,128)(2,1)S(1)}, u32[]{:S(2)}, u32[]{:S(2)}) collective-permute-start(bf16[18,64,128]{2,1,0:T(8,128)(2,1)S(1)} %local_rest.3.after_ref.own_ref), channel_id=1, source_target_pairs={{0,1},{1,0},{2,3},{3,2},{4,5},{5,4},{6,7},{7,6},{8,9},{9,8},{10,11... | collective-permute-start | bytes 884744 | tf_op jit(solution)/shard_map/ppermute | solution.py:259
  10.9 6.2 %collective-permute-start.5 = (bf16[9,64,128]{2,1,0:T(8,128)(2,1)S(1)}, bf16[9,64,128]{2,1,0:T(8,128)(2,1)S(1)}, u32[]{:S(2)}, u32[]{:S(2)}) collective-permute-start(bf16[9,64,128]{2,1,0:T(8,128)(2,1)S(1)} %cross_level.17.after_ref.own_ref), channel_id=1, source_target_pairs={{0,2},{1,3},{2,0},{3,1},{4,6},{5,7},{6,4},{7,5},{8,10},{9,11},{10,... | collective-permute-start | bytes 442376 | tf_op jit(solution)/shard_map/ppermute | solution.py:259
  13.4 6.0 %collective-permute-start.4 = (bf16[5,64,128]{2,1,0:T(8,128)(2,1)S(1)}, bf16[5,64,128]{2,1,0:T(8,128)(2,1)S(1)}, u32[]{:S(2)}, u32[]{:S(2)}) collective-permute-start(bf16[5,64,128]{2,1,0:T(8,128)(2,1)S(1)} %cross_level.18.after_ref.own_ref), channel_id=1, source_target_pairs={{0,4},{4,0},{8,12},{12,8},{16,20},{20,16},{24,28},{28,24},{1,5},{5... | collective-permute-start | bytes 245768 | tf_op jit(solution)/shard_map/ppermute | solution.py:259
  15.4 4.0 %copy-start = (bf16[64,3,64,128]{3,2,1,0:T(8,128)(2,1)S(1)}, bf16[64,3,64,128]{3,2,1,0:T(8,128)(2,1)}, u32[]{:S(2)}) copy-start(bf16[64,3,64,128]{3,2,1,0:T(8,128)(2,1)} %mix_ref.23) | copy-start | bytes 9437188
  15.4 7.2 %collective-permute-start.7 = (bf16[10,64,128]{2,1,0:T(8,128)(2,1)S(1)}, bf16[10,64,128]{2,1,0:T(8,128)(2,1)S(1)}, u32[]{:S(2)}, u32[]{:S(2)}) collective-permute-start(bf16[10,64,128]{2,1,0:T(8,128)(2,1)S(1)} %cross_level.19.after_ref.own_ref), channel_id=1, source_target_pairs={{0,2},{1,3},{2,0},{3,1},{4,6},{5,7},{6,4},{7,5},{8,10},{9,11},{10,... | collective-permute-start | bytes 491528 | tf_op jit(solution)/shard_map/ppermute | solution.py:259
  17.4 6.2 %collective-permute-start.10 = (bf16[9,64,128]{2,1,0:T(8,128)(2,1)S(1)}, bf16[9,64,128]{2,1,0:T(8,128)(2,1)S(1)}, u32[]{:S(2)}, u32[]{:S(2)}) collective-permute-start(bf16[9,64,128]{2,1,0:T(8,128)(2,1)S(1)} %cross_level.20.after_ref.own_ref), channel_id=1, source_target_pairs={{0,4},{4,0},{8,12},{12,8},{16,20},{20,16},{24,28},{28,24},{1,5},{5... | collective-permute-start | bytes 442376 | tf_op jit(solution)/shard_map/ppermute | solution.py:259
  19.6 5.2 %collective-permute-start.9 = (bf16[5,64,128]{2,1,0:T(8,128)(2,1)S(1)}, bf16[5,64,128]{2,1,0:T(8,128)(2,1)S(1)}, u32[]{:S(2)}, u32[]{:S(2)}) collective-permute-start(bf16[5,64,128]{2,1,0:T(8,128)(2,1)S(1)} %cross_level.21.after_ref.own_ref), channel_id=1, source_target_pairs={{0,8},{4,12},{8,0},{12,4},{16,24},{20,28},{24,16},{28,20},{1,9},{5... | collective-permute-start | bytes 245768 | tf_op jit(solution)/shard_map/ppermute | solution.py:259
  21.4 7.7 %collective-permute-start.6 = (bf16[8,64,128]{2,1,0:T(8,128)(2,1)S(1)}, bf16[8,64,128]{2,1,0:T(8,128)(2,1)S(1)}, u32[]{:S(2)}, u32[]{:S(2)}) collective-permute-start(bf16[8,64,128]{2,1,0:T(8,128)(2,1)S(1)} %cross_level.22.after_ref.own_ref), channel_id=1, source_target_pairs={{0,2},{1,3},{2,0},{3,1},{4,6},{5,7},{6,4},{7,5},{8,10},{9,11},{10,... | collective-permute-start | bytes 393224 | tf_op jit(solution)/shard_map/ppermute | solution.py:259
  22.8 5.4 %collective-permute-start.8 = (bf16[10,64,128]{2,1,0:T(8,128)(2,1)S(1)}, bf16[10,64,128]{2,1,0:T(8,128)(2,1)S(1)}, u32[]{:S(2)}, u32[]{:S(2)}) collective-permute-start(bf16[10,64,128]{2,1,0:T(8,128)(2,1)S(1)} %cross_level.23.after_ref.own_ref), channel_id=1, source_target_pairs={{0,4},{4,0},{8,12},{12,8},{16,20},{20,16},{24,28},{28,24},{1,5},{5... | collective-permute-start | bytes 491528 | tf_op jit(solution)/shard_map/ppermute | solution.py:259
  23.8 7.2 %collective-permute-start.12 = (bf16[9,64,128]{2,1,0:T(8,128)(2,1)S(1)}, bf16[9,64,128]{2,1,0:T(8,128)(2,1)S(1)}, u32[]{:S(2)}, u32[]{:S(2)}) collective-permute-start(bf16[9,64,128]{2,1,0:T(8,128)(2,1)S(1)} %cross_level.24.after_ref.own_ref), channel_id=1, source_target_pairs={{0,8},{4,12},{8,0},{12,4},{16,24},{20,28},{24,16},{28,20},{1,9},{5... | collective-permute-start | bytes 442376 | tf_op jit(solution)/shard_map/ppermute | solution.py:259
  25.0 19.4 %collective-permute-start.18 = (bf16[5,64,128]{2,1,0:T(8,128)(2,1)S(1)}, bf16[5,64,128]{2,1,0:T(8,128)(2,1)S(1)}, u32[]{:S(2)}, u32[]{:S(2)}) collective-permute-start(bf16[5,64,128]{2,1,0:T(8,128)(2,1)S(1)} %cross_level.25.after_ref.own_ref), channel_id=1, source_target_pairs={{0,16},{4,20},{8,24},{12,28},{16,0},{20,4},{24,8},{28,12},{1,17},{... | collective-permute-start | bytes 245768 | tf_op jit(solution)/shard_map/ppermute | solution.py:259
  28.5 10.0 %collective-permute-start.14 = (bf16[10,64,128]{2,1,0:T(8,128)(2,1)S(1)}, bf16[10,64,128]{2,1,0:T(8,128)(2,1)S(1)}, u32[]{:S(2)}, u32[]{:S(2)}) collective-permute-start(bf16[10,64,128]{2,1,0:T(8,128)(2,1)S(1)} %cross_level.26.after_ref.own_ref), channel_id=1, source_target_pairs={{0,8},{4,12},{8,0},{12,4},{16,24},{20,28},{24,16},{28,20},{1,9},{5... | collective-permute-start | bytes 491528 | tf_op jit(solution)/shard_map/ppermute | solution.py:259
  29.3 5.0 %collective-permute-start.11 = (bf16[8,64,128]{2,1,0:T(8,128)(2,1)S(1)}, bf16[8,64,128]{2,1,0:T(8,128)(2,1)S(1)}, u32[]{:S(2)}, u32[]{:S(2)}) collective-permute-start(bf16[8,64,128]{2,1,0:T(8,128)(2,1)S(1)} %cross_level.27.after_ref.own_ref), channel_id=1, source_target_pairs={{0,4},{4,0},{8,12},{12,8},{16,20},{20,16},{24,28},{28,24},{1,5},{5... | collective-permute-start | bytes 393224 | tf_op jit(solution)/shard_map/ppermute | solution.py:259
  31.2 14.2 %collective-permute-start.17 = (bf16[9,64,128]{2,1,0:T(8,128)(2,1)S(1)}, bf16[9,64,128]{2,1,0:T(8,128)(2,1)S(1)}, u32[]{:S(2)}, u32[]{:S(2)}) collective-permute-start(bf16[9,64,128]{2,1,0:T(8,128)(2,1)S(1)} %cross_level.28.after_ref.own_ref), channel_id=1, source_target_pairs={{0,16},{4,20},{8,24},{12,28},{16,0},{20,4},{24,8},{28,12},{1,17},{... | collective-permute-start | bytes 442376 | tf_op jit(solution)/shard_map/ppermute | solution.py:259
  34.6 6.1 %collective-permute-start.13 = (bf16[8,64,128]{2,1,0:T(8,128)(2,1)S(1)}, bf16[8,64,128]{2,1,0:T(8,128)(2,1)S(1)}, u32[]{:S(2)}, u32[]{:S(2)}) collective-permute-start(bf16[8,64,128]{2,1,0:T(8,128)(2,1)S(1)} %cross_level.29.after_ref.own_ref), channel_id=1, source_target_pairs={{0,8},{4,12},{8,0},{12,4},{16,24},{20,28},{24,16},{28,20},{1,9},{5... | collective-permute-start | bytes 393224 | tf_op jit(solution)/shard_map/ppermute | solution.py:259
  38.8 5.6 %copy-start.1 = (bf16[64,64,256]{2,1,0:T(8,128)(2,1)S(1)}, bf16[64,64,256]{2,1,0:T(8,128)(2,1)}, u32[]{:S(2)}) copy-start(bf16[64,64,256]{2,1,0:T(8,128)(2,1)} %leaf_ref.7) | copy-start | bytes 6291460
  38.8 12.1 %collective-permute-start.16 = (bf16[10,64,128]{2,1,0:T(8,128)(2,1)S(1)}, bf16[10,64,128]{2,1,0:T(8,128)(2,1)S(1)}, u32[]{:S(2)}, u32[]{:S(2)}) collective-permute-start(bf16[10,64,128]{2,1,0:T(8,128)(2,1)S(1)} %cross_level.30.after_ref.own_ref), channel_id=1, source_target_pairs={{0,16},{4,20},{8,24},{12,28},{16,0},{20,4},{24,8},{28,12},{1,17},{... | collective-permute-start | bytes 491528 | tf_op jit(solution)/shard_map/ppermute | solution.py:259
  40.9 11.4 %collective-permute-start.15 = (bf16[8,64,128]{2,1,0:T(8,128)(2,1)S(1)}, bf16[8,64,128]{2,1,0:T(8,128)(2,1)S(1)}, u32[]{:S(2)}, u32[]{:S(2)}) collective-permute-start(bf16[8,64,128]{2,1,0:T(8,128)(2,1)S(1)} %cross_level.31.rest_0_.own_ref), channel_id=1, source_target_pairs={{0,16},{4,20},{8,24},{12,28},{16,0},{20,4},{24,8},{28,12},{1,17},{... | collective-permute-start | bytes 393224 | tf_op jit(solution)/shard_map/ppermute | solution.py:259

commit v2 on v1

--- a/solution.py
+++ b/solution.py
@@ -8,8 +8,8 @@
 from jax.sharding import PartitionSpec as P
 
 NT = (((1,), (1,)), ((), ()))
-PIECES = 4
-SHARES = (5, 9, 10, 8)
+PIECES = 8
+SHARES = (5, 8, 10, 9)
 LAGS = (
     (1.0, 1.1, 1.2, 1.3),
     (0.0, 0.5, 1.2, 1.6),
@@ -44,11 +44,9 @@
     src_hbm,
     leaf_hbm,
     mix_hbm,
-    lo_hbm,
     first,
     state,
     last_mix,
-    lo_mix,
     even,
     odd,
     src,
@@ -57,7 +55,6 @@
     src_sem,
     leaf_sem,
     mix_sem,
-    lo_sem,
 ):
     pairs = even.shape[0]
     blocks = leaf.shape[0]
@@ -77,7 +74,6 @@
         held = mix.at[level] if level < levels - 1 else last_mix
         return pltpu.make_async_copy(mix_hbm.at[:, level], held, mix_sem.at[level])
 
-    next_levels = pltpu.make_async_copy(lo_hbm, lo_mix, lo_sem)
     for piece in range(PIECES):
         for copy in inputs(piece):
             copy.start()
@@ -97,7 +93,6 @@
                 preferred_element_type=jnp.float32,
             )
             even[pair] = pack(product).astype(even.dtype)
-    next_levels.start()
 
     for level in range(levels):
         factors(level).wait()
@@ -112,10 +107,9 @@
             chosen = last_mix if level == levels - 1 else mix.at[level]
             part = chosen[2 * pair : 2 * pair + 2]
             new[pair] = mix_pair(own, other, part).astype(own.dtype)
-    next_levels.wait()
-
-
-def local_phase(sources, leaf_in, local_mix, lo_mix, size):
+
+
+def local_phase(sources, leaf_in, local_mix, size):
     vectors = sources.shape[0]
     blocks, rank, _ = leaf_in.shape
     levels = local_mix.shape[1]
@@ -125,10 +119,9 @@
             pltpu.VMEM((size, rank, 2 * vectors), jnp.bfloat16),
             pltpu.VMEM((blocks // 2, rank, 2 * vectors), jnp.bfloat16),
             pltpu.VMEM((blocks,) + local_mix.shape[2:], local_mix.dtype),
-            pltpu.VMEM(lo_mix.shape, lo_mix.dtype),
         ],
-        in_specs=[pl.BlockSpec(memory_space=pltpu.HBM)] * 4,
-        out_specs=[pl.BlockSpec(memory_space=pltpu.VMEM)] * 4,
+        in_specs=[pl.BlockSpec(memory_space=pltpu.HBM)] * 3,
+        out_specs=[pl.BlockSpec(memory_space=pltpu.VMEM)] * 3,
         scratch_shapes=[
             pltpu.VMEM((blocks // 2, rank, 2 * vectors), jnp.bfloat16),
             pltpu.VMEM((blocks // 2, rank, 2 * vectors), jnp.bfloat16),
@@ -138,12 +131,11 @@
             pltpu.SemaphoreType.DMA((PIECES,)),
             pltpu.SemaphoreType.DMA((PIECES,)),
             pltpu.SemaphoreType.DMA((levels,)),
-            pltpu.SemaphoreType.DMA,
         ],
         compiler_params=pltpu.CompilerParams(vmem_limit_bytes=58 << 20),
         cost_estimate=pl.CostEstimate(flops=10**9, bytes_accessed=10 << 20, transcendentals=0),
         name="local_levels",
-    )(sources, leaf_in, local_mix, lo_mix)
+    )(sources, leaf_in, local_mix)
 
 
 def rest_kernel(start, state_ref, mix_ref, after_ref, out_ref):
@@ -280,8 +272,7 @@
         lags = LAGS[min(end - s, 3) if s else 4]
         return s + lags[c], -s
 
-    first, state, last_mix, lo_mix = local_phase(sources, leaf_in, local_mix, lo_mix, head)
-    steps[:lo_levels] = [("lo", n, lo_mix) for n in range(lo_levels)]
+    first, state, last_mix = local_phase(sources, leaf_in, local_mix, head)
     axis, level, _ = steps[0]
     waiting[0, 0] = first, swapped(first, axis, level), 0
     after = state

time: 53.7 us -> 53.8 us (level)
  transfers between devices with their start and end apart: 19 -> 19, of which waited for: 10 -> 9; matrix products, arithmetic and copies ran while one was open for 0% -> 0% of each run, Pallas kernels for 14% -> 14%
where the time goes in v2:
time: 53.8 us; the launch traced here: 53.6 us
  starting transfers between devices  26.7 us (50%)
  Pallas kernels  14.7 us (27%)
  waiting for transfers between devices  12 us (22%)
    ppermute x19, starting transfers between devices, swapped(): return lax.ppermute(block, axis, route)  26.7 us
    ppermute x19, waiting for transfers between devices, swapped(): return lax.ppermute(block, axis, route)  12 us
    pallas_call x1, Pallas kernels, local_phase(): pl.pallas_call(local_kernel, out_shape=[pltpu.VMEM((size, rank, 2 * vecto...  5.67 us
    pallas_call x4, Pallas kernels, final_level(): pl.pallas_call(functools.partial(final_kernel, has_token, level, start),...  4.99 us
    pallas_call x16, Pallas kernels, cross_level(): pl.pallas_call(functools.partial(cross_kernel, level, start, offset), out...  3.55 us
  transfers between devices with their start and end apart: 19, of which 9 were waited for; matrix products, arithmetic and copies ran while one was open for 0% of the time, Pallas kernels for 14%

profile of v2, /device:TPU:0, one launch (start us, length us, event | category | flops | bytes accessed | tf_op | source)
XLA Modules:
  0.0 53.6 jit_solution(18187769268050308980)
XLA Ops:
  0.0 5.7 %local_levels.1 = (bf16[5,64,128]{2,1,0:T(8,128)(2,1)S(1)}, bf16[32,64,128]{2,1,0:T(8,128)(2,1)S(1)}, bf16[64,64,128]{2,1,0:T(8,128)(2,1)S(1)}) custom-call(bf16[64,16384]{1,0:T(8,128)(2,1)} %src_hbm.1, bf16[64,64,256]{2,1,0:T(8,128)(2,1)} %leaf_hbm.1, bf16[64,6,64,128]{3,2,1,0:T(8,128)(2,1)} %mix_hbm.1), custom_call_target="tpu_custom_call" | custom-call | flops 1000000000 | bytes 10485760 | tf_op jit(solution)/shard_map/local_levels/pallas_call | solution.py:116
  5.7 0.5 collective-permute-start
  6.2 0.9 %collective-permute-done.other_ref = bf16[5,64,128]{2,1,0:T(8,128)(2,1)S(1)} collective-permute-done((bf16[5,64,128]{2,1,0:T(8,128)(2,1)S(1)}, bf16[5,64,128]{2,1,0:T(8,128)(2,1)S(1)}, u32[]{:S(2)}, u32[]{:S(2)}) %collective-permute-start) | collective-permute-done | bytes 81952 | tf_op jit(solution)/shard_map/ppermute | solution.py:251
  7.3 0.2 local_rest.2.own_ref.after_ref
  7.5 0.4 collective-permute-start.1
  8.0 2.7 %collective-permute-start.3 = (bf16[5,64,128]{2,1,0:T(8,128)(2,1)S(1)}, bf16[5,64,128]{2,1,0:T(8,128)(2,1)S(1)}, u32[]{:S(2)}, u32[]{:S(2)}) collective-permute-start(bf16[5,64,128]{2,1,0:T(8,128)(2,1)S(1)} %cross_level.16.after_ref.own_ref), channel_id=1, source_target_pairs={{0,2},{1,3},{2,0},{3,1},{4,6},{5,7},{6,4},{7,5},{8,10},{9,11},{10,... | collective-permute-start | bytes 245768 | tf_op jit(solution)/shard_map/ppermute | solution.py:251
  10.6 0.2 cross_level.17.after_ref.own_ref
  10.9 0.3 local_rest.3.after_ref.own_ref
  11.3 1.3 %collective-permute-start.5 = (bf16[8,64,128]{2,1,0:T(8,128)(2,1)S(1)}, bf16[8,64,128]{2,1,0:T(8,128)(2,1)S(1)}, u32[]{:S(2)}, u32[]{:S(2)}) collective-permute-start(bf16[8,64,128]{2,1,0:T(8,128)(2,1)S(1)} %cross_level.17.after_ref.own_ref), channel_id=1, source_target_pairs={{0,2},{1,3},{2,0},{3,1},{4,6},{5,7},{6,4},{7,5},{8,10},{9,11},{10,... | collective-permute-start | bytes 393224 | tf_op jit(solution)/shard_map/ppermute | solution.py:251
  12.6 1.0 %collective-permute-done.3.other_ref = bf16[5,64,128]{2,1,0:T(8,128)(2,1)S(1)} collective-permute-done((bf16[5,64,128]{2,1,0:T(8,128)(2,1)S(1)}, bf16[5,64,128]{2,1,0:T(8,128)(2,1)S(1)}, u32[]{:S(2)}, u32[]{:S(2)}) %collective-permute-start.3) | collective-permute-done | bytes 81952 | tf_op jit(solution)/shard_map/ppermute | solution.py:251
  13.8 1.8 %collective-permute-start.4 = (bf16[5,64,128]{2,1,0:T(8,128)(2,1)S(1)}, bf16[5,64,128]{2,1,0:T(8,128)(2,1)S(1)}, u32[]{:S(2)}, u32[]{:S(2)}) collective-permute-start(bf16[5,64,128]{2,1,0:T(8,128)(2,1)S(1)} %cross_level.18.after_ref.own_ref), channel_id=1, source_target_pairs={{0,4},{4,0},{8,12},{12,8},{16,20},{20,16},{24,28},{28,24},{1,5},{5... | collective-permute-start | bytes 245768 | tf_op jit(solution)/shard_map/ppermute | solution.py:251
  15.6 0.2 cross_level.19.after_ref.own_ref
  15.8 1.6 %collective-permute-start.7 = (bf16[10,64,128]{2,1,0:T(8,128)(2,1)S(1)}, bf16[10,64,128]{2,1,0:T(8,128)(2,1)S(1)}, u32[]{:S(2)}, u32[]{:S(2)}) collective-permute-start(bf16[10,64,128]{2,1,0:T(8,128)(2,1)S(1)} %cross_level.19.after_ref.own_ref), channel_id=1, source_target_pairs={{0,2},{1,3},{2,0},{3,1},{4,6},{5,7},{6,4},{7,5},{8,10},{9,11},{10,... | collective-permute-start | bytes 491528 | tf_op jit(solution)/shard_map/ppermute | solution.py:251
  17.4 0.2 cross_level.20.after_ref.own_ref
  17.6 1.6 %collective-permute-start.10 = (bf16[8,64,128]{2,1,0:T(8,128)(2,1)S(1)}, bf16[8,64,128]{2,1,0:T(8,128)(2,1)S(1)}, u32[]{:S(2)}, u32[]{:S(2)}) collective-permute-start(bf16[8,64,128]{2,1,0:T(8,128)(2,1)S(1)} %cross_level.20.after_ref.own_ref), channel_id=1, source_target_pairs={{0,4},{4,0},{8,12},{12,8},{16,20},{20,16},{24,28},{28,24},{1,5},{5... | collective-permute-start | bytes 393224 | tf_op jit(solution)/shard_map/ppermute | solution.py:251
  19.3 0.2 cross_level.21.after_ref.own_ref
  19.5 1.7 %collective-permute-start.9 = (bf16[5,64,128]{2,1,0:T(8,128)(2,1)S(1)}, bf16[5,64,128]{2,1,0:T(8,128)(2,1)S(1)}, u32[]{:S(2)}, u32[]{:S(2)}) collective-permute-start(bf16[5,64,128]{2,1,0:T(8,128)(2,1)S(1)} %cross_level.21.after_ref.own_ref), channel_id=1, source_target_pairs={{0,8},{4,12},{8,0},{12,4},{16,24},{20,28},{24,16},{28,20},{1,9},{5... | collective-permute-start | bytes 245768 | tf_op jit(solution)/shard_map/ppermute | solution.py:251
  21.1 0.2 cross_level.22.after_ref.own_ref
  21.4 0.9 %collective-permute-start.6 = (bf16[9,64,128]{2,1,0:T(8,128)(2,1)S(1)}, bf16[9,64,128]{2,1,0:T(8,128)(2,1)S(1)}, u32[]{:S(2)}, u32[]{:S(2)}) collective-permute-start(bf16[9,64,128]{2,1,0:T(8,128)(2,1)S(1)} %cross_level.22.after_ref.own_ref), channel_id=1, source_target_pairs={{0,2},{1,3},{2,0},{3,1},{4,6},{5,7},{6,4},{7,5},{8,10},{9,11},{10,... | collective-permute-start | bytes 442376 | tf_op jit(solution)/shard_map/ppermute | solution.py:251
  22.3 0.2 cross_level.23.after_ref.own_ref
  22.5 1.5 %collective-permute-start.8 = (bf16[10,64,128]{2,1,0:T(8,128)(2,1)S(1)}, bf16[10,64,128]{2,1,0:T(8,128)(2,1)S(1)}, u32[]{:S(2)}, u32[]{:S(2)}) collective-permute-start(bf16[10,64,128]{2,1,0:T(8,128)(2,1)S(1)} %cross_level.23.after_ref.own_ref), channel_id=1, source_target_pairs={{0,4},{4,0},{8,12},{12,8},{16,20},{20,16},{24,28},{28,24},{1,5},{5... | collective-permute-start | bytes 491528 | tf_op jit(solution)/shard_map/ppermute | solution.py:251
  24.0 0.2 cross_level.24.after_ref.own_ref
  24.2 0.5 collective-permute-start.12
  24.7 0.2 cross_level.25.after_ref.own_ref
  24.9 2.6 %collective-permute-start.18 = (bf16[5,64,128]{2,1,0:T(8,128)(2,1)S(1)}, bf16[5,64,128]{2,1,0:T(8,128)(2,1)S(1)}, u32[]{:S(2)}, u32[]{:S(2)}) collective-permute-start(bf16[5,64,128]{2,1,0:T(8,128)(2,1)S(1)} %cross_level.25.after_ref.own_ref), channel_id=1, source_target_pairs={{0,16},{4,20},{8,24},{12,28},{16,0},{20,4},{24,8},{28,12},{1,17},{... | collective-permute-start | bytes 245768 | tf_op jit(solution)/shard_map/ppermute | solution.py:251
  27.6 0.3 collective-permute-done.8.other_ref
  27.9 0.2 cross_level.26.after_ref.own_ref
  28.2 1.3 %collective-permute-start.14 = (bf16[10,64,128]{2,1,0:T(8,128)(2,1)S(1)}, bf16[10,64,128]{2,1,0:T(8,128)(2,1)S(1)}, u32[]{:S(2)}, u32[]{:S(2)}) collective-permute-start(bf16[10,64,128]{2,1,0:T(8,128)(2,1)S(1)} %cross_level.26.after_ref.own_ref), channel_id=1, source_target_pairs={{0,8},{4,12},{8,0},{12,4},{16,24},{20,28},{24,16},{28,20},{1,9},{5... | collective-permute-start | bytes 491528 | tf_op jit(solution)/shard_map/ppermute | solution.py:251
  29.5 0.2 cross_level.27.after_ref.own_ref
  29.7 0.7 %collective-permute-start.11 = (bf16[9,64,128]{2,1,0:T(8,128)(2,1)S(1)}, bf16[9,64,128]{2,1,0:T(8,128)(2,1)S(1)}, u32[]{:S(2)}, u32[]{:S(2)}) collective-permute-start(bf16[9,64,128]{2,1,0:T(8,128)(2,1)S(1)} %cross_level.27.after_ref.own_ref), channel_id=1, source_target_pairs={{0,4},{4,0},{8,12},{12,8},{16,20},{20,16},{24,28},{28,24},{1,5},{5... | collective-permute-start | bytes 442376 | tf_op jit(solution)/shard_map/ppermute | solution.py:251
  30.4 0.3 collective-permute-done.12.other_ref
  30.7 0.2 cross_level.28.after_ref.own_ref
  31.0 2.3 %collective-permute-start.17 = (bf16[8,64,128]{2,1,0:T(8,128)(2,1)S(1)}, bf16[8,64,128]{2,1,0:T(8,128)(2,1)S(1)}, u32[]{:S(2)}, u32[]{:S(2)}) collective-permute-start(bf16[8,64,128]{2,1,0:T(8,128)(2,1)S(1)} %cross_level.28.after_ref.own_ref), channel_id=1, source_target_pairs={{0,16},{4,20},{8,24},{12,28},{16,0},{20,4},{24,8},{28,12},{1,17},{... | collective-permute-start | bytes 393224 | tf_op jit(solution)/shard_map/ppermute | solution.py:251
  33.3 1.7 %collective-permute-done.11.other_ref = bf16[9,64,128]{2,1,0:T(8,128)(2,1)S(1)} collective-permute-done((bf16[9,64,128]{2,1,0:T(8,128)(2,1)S(1)}, bf16[9,64,128]{2,1,0:T(8,128)(2,1)S(1)}, u32[]{:S(2)}, u32[]{:S(2)}) %collective-permute-start.11) | collective-permute-done | bytes 147488 | tf_op jit(solution)/shard_map/ppermute | solution.py:251
  34.9 0.2 cross_level.29.after_ref.own_ref
  35.2 0.8 %collective-permute-start.13 = (bf16[9,64,128]{2,1,0:T(8,128)(2,1)S(1)}, bf16[9,64,128]{2,1,0:T(8,128)(2,1)S(1)}, u32[]{:S(2)}, u32[]{:S(2)}) collective-permute-start(bf16[9,64,128]{2,1,0:T(8,128)(2,1)S(1)} %cross_level.29.after_ref.own_ref), channel_id=1, source_target_pairs={{0,8},{4,12},{8,0},{12,4},{16,24},{20,28},{24,16},{28,20},{1,9},{5... | collective-permute-start | bytes 442376 | tf_op jit(solution)/shard_map/ppermute | solution.py:251
  36.0 0.8 %collective-permute-done.14.other_ref = bf16[10,64,128]{2,1,0:T(8,128)(2,1)S(1)} collective-permute-done((bf16[10,64,128]{2,1,0:T(8,128)(2,1)S(1)}, bf16[10,64,128]{2,1,0:T(8,128)(2,1)S(1)}, u32[]{:S(2)}, u32[]{:S(2)}) %collective-permute-start.14) | collective-permute-done | bytes 163872 | tf_op jit(solution)/shard_map/ppermute | solution.py:251
  36.8 0.2 cross_level.30.after_ref.own_ref
  37.1 1.9 %collective-permute-start.16 = (bf16[10,64,128]{2,1,0:T(8,128)(2,1)S(1)}, bf16[10,64,128]{2,1,0:T(8,128)(2,1)S(1)}, u32[]{:S(2)}, u32[]{:S(2)}) collective-permute-start(bf16[10,64,128]{2,1,0:T(8,128)(2,1)S(1)} %cross_level.30.after_ref.own_ref), channel_id=1, source_target_pairs={{0,16},{4,20},{8,24},{12,28},{16,0},{20,4},{24,8},{28,12},{1,17},{... | collective-permute-start | bytes 491528 | tf_op jit(solution)/shard_map/ppermute | solution.py:251
  38.9 2.6 %collective-permute-done.13.other_ref = bf16[9,64,128]{2,1,0:T(8,128)(2,1)S(1)} collective-permute-done((bf16[9,64,128]{2,1,0:T(8,128)(2,1)S(1)}, bf16[9,64,128]{2,1,0:T(8,128)(2,1)S(1)}, u32[]{:S(2)}, u32[]{:S(2)}) %collective-permute-start.13) | collective-permute-done | bytes 147488 | tf_op jit(solution)/shard_map/ppermute | solution.py:251
  41.6 0.2 cross_level.31.rest_0_.own_ref
  41.8 2.4 %collective-permute-start.15 = (bf16[9,64,128]{2,1,0:T(8,128)(2,1)S(1)}, bf16[9,64,128]{2,1,0:T(8,128)(2,1)S(1)}, u32[]{:S(2)}, u32[]{:S(2)}) collective-permute-start(bf16[9,64,128]{2,1,0:T(8,128)(2,1)S(1)} %cross_level.31.rest_0_.own_ref), channel_id=1, source_target_pairs={{0,16},{4,20},{8,24},{12,28},{16,0},{20,4},{24,8},{28,12},{1,17},{... | collective-permute-start | bytes 442376 | tf_op jit(solution)/shard_map/ppermute | solution.py:251
  44.2 1.1 %final_level.4 = (bf16[64,16384]{1,0:T(8,128)(2,1)}, f32[8,128]{1,0:T(8,128)S(1)}) custom-call(bf16[5,64,128]{2,1,0:T(8,128)(2,1)S(1)} %cross_level.25.after_ref.own_ref, bf16[5,64,128]{2,1,0:T(8,128)(2,1)S(1)} %collective-permute-done.18.other_ref, bf16[64,3,64,128]{3,2,1,0:T(8,128)(2,1)S(1)} %copy-done, bf16[64,64,256]{2,1,0:T(8,128)(2,1)S(1)} %copy-done.2, ...), custom_call_target="tpu_custom_call" | custom-call | flops 3000000000 | tf_op jit(solution)/shard_map/final_level/pallas_call | solution.py:230
  45.4 1.3 %final_level.5 = (bf16[64,16384]{1,0:T(8,128)(2,1)}, f32[8,128]{1,0:T(8,128)S(1)}) custom-call(bf16[8,64,128]{2,1,0:T(8,128)(2,1)S(1)} %cross_level.28.after_ref.own_ref, bf16[8,64,128]{2,1,0:T(8,128)(2,1)S(1)} %collective-permute-done.17.other_ref, bf16[64,3,64,128]{3,2,1,0:T(8,128)(2,1)S(1)} %copy-done, ...), custom_call_target="tpu_custom_call", output_to_operand_aliasing={{0}: (5, {})} | custom-call | flops 3000000000 | tf_op jit(solution)/shard_map/final_level/pallas_call | solution.py:230
  46.7 3.9 %collective-permute-done.16.other_ref = bf16[10,64,128]{2,1,0:T(8,128)(2,1)S(1)} collective-permute-done((bf16[10,64,128]{2,1,0:T(8,128)(2,1)S(1)}, bf16[10,64,128]{2,1,0:T(8,128)(2,1)S(1)}, u32[]{:S(2)}, u32[]{:S(2)}) %collective-permute-start.16) | collective-permute-done | bytes 163872 | tf_op jit(solution)/shard_map/ppermute | solution.py:251
  50.6 1.3 %final_level.6 = (bf16[64,16384]{1,0:T(8,128)(2,1)}, f32[8,128]{1,0:T(8,128)S(1)}) custom-call(bf16[10,64,128]{2,1,0:T(8,128)(2,1)S(1)} %cross_level.30.after_ref.own_ref, bf16[10,64,128]{2,1,0:T(8,128)(2,1)S(1)} %collective-permute-done.16.other_ref, bf16[64,3,64,128]{3,2,1,0:T(8,128)(2,1)S(1)} %copy-done, ...), custom_call_target="tpu_custom_call", output_to_operand_aliasing={{0}: (5, {})} | custom-call | flops 3000000000 | tf_op jit(solution)/shard_map/final_level/pallas_call | solution.py:230
  51.9 0.4 collective-permute-done.15.other_ref
  52.3 1.3 %final_level.7 = bf16[64,16384]{1,0:T(8,128)(2,1)} custom-call(bf16[9,64,128]{2,1,0:T(8,128)(2,1)S(1)} %cross_level.31.rest_0_.own_ref, bf16[9,64,128]{2,1,0:T(8,128)(2,1)S(1)} %collective-permute-done.15.other_ref, bf16[64,3,64,128]{3,2,1,0:T(8,128)(2,1)S(1)} %copy-done, bf16[64,64,256]{2,1,0:T(8,128)(2,1)S(1)} %copy-done.2, ...), custom_call_target="tpu_custom_call", output_to_operand_aliasing={{}: (5, {})} | custom-call | flops 3000000000 | tf_op jit(solution)/shard_map/final_level/pallas_call | solution.py:230
  (19 shorter events, 0.6 us)
Async XLA Ops:
  0.0 7.1 %copy-start.1 = (bf16[64,2,64,128]{3,2,1,0:T(8,128)(2,1)S(1)}, bf16[64,2,64,128]{3,2,1,0:T(8,128)(2,1)}, u32[]{:S(2)}) copy-start(bf16[64,2,64,128]{3,2,1,0:T(8,128)(2,1)} %mix_ref.31) | copy-start | bytes 6291460
  5.7 1.4 %collective-permute-start = (bf16[5,64,128]{2,1,0:T(8,128)(2,1)S(1)}, bf16[5,64,128]{2,1,0:T(8,128)(2,1)S(1)}, u32[]{:S(2)}, u32[]{:S(2)}) collective-permute-start(bf16[5,64,128]{2,1,0:T(8,128)(2,1)S(1)} %get-tuple-element.16.own_ref), channel_id=1, source_target_pairs={{0,1},{1,0},{2,3},{3,2},{4,5},{5,4},{6,7},{7,6},{8,9},{9,8},{10,11... | collective-permute-start | bytes 245768 | tf_op jit(solution)/shard_map/ppermute | solution.py:251
  7.5 3.1 %collective-permute-start.1 = (bf16[8,64,128]{2,1,0:T(8,128)(2,1)S(1)}, bf16[8,64,128]{2,1,0:T(8,128)(2,1)S(1)}, u32[]{:S(2)}, u32[]{:S(2)}) collective-permute-start(bf16[8,64,128]{2,1,0:T(8,128)(2,1)S(1)} %local_rest.2.own_ref.after_ref), channel_id=1, source_target_pairs={{0,1},{1,0},{2,3},{3,2},{4,5},{5,4},{6,7},{7,6},{8,9},{9,8},{10,11... | collective-permute-start | bytes 393224 | tf_op jit(solution)/shard_map/ppermute | solution.py:251
  8.0 5.6 %collective-permute-start.3 = (bf16[5,64,128]{2,1,0:T(8,128)(2,1)S(1)}, bf16[5,64,128]{2,1,0:T(8,128)(2,1)S(1)}, u32[]{:S(2)}, u32[]{:S(2)}) collective-permute-start(bf16[5,64,128]{2,1,0:T(8,128)(2,1)S(1)} %cross_level.16.after_ref.own_ref), channel_id=1, source_target_pairs={{0,2},{1,3},{2,0},{3,1},{4,6},{5,7},{6,4},{7,5},{8,10},{9,11},{10,... | collective-permute-start | bytes 245768 | tf_op jit(solution)/shard_map/ppermute | solution.py:251
  11.2 4.4 %collective-permute-start.2 = (bf16[19,64,128]{2,1,0:T(8,128)(2,1)S(1)}, bf16[19,64,128]{2,1,0:T(8,128)(2,1)S(1)}, u32[]{:S(2)}, u32[]{:S(2)}) collective-permute-start(bf16[19,64,128]{2,1,0:T(8,128)(2,1)S(1)} %local_rest.3.after_ref.own_ref), channel_id=1, source_target_pairs={{0,1},{1,0},{2,3},{3,2},{4,5},{5,4},{6,7},{7,6},{8,9},{9,8},{10,11... | collective-permute-start | bytes 933896 | tf_op jit(solution)/shard_map/ppermute | solution.py:251
  11.3 6.1 %collective-permute-start.5 = (bf16[8,64,128]{2,1,0:T(8,128)(2,1)S(1)}, bf16[8,64,128]{2,1,0:T(8,128)(2,1)S(1)}, u32[]{:S(2)}, u32[]{:S(2)}) collective-permute-start(bf16[8,64,128]{2,1,0:T(8,128)(2,1)S(1)} %cross_level.17.after_ref.own_ref), channel_id=1, source_target_pairs={{0,2},{1,3},{2,0},{3,1},{4,6},{5,7},{6,4},{7,5},{8,10},{9,11},{10,... | collective-permute-start | bytes 393224 | tf_op jit(solution)/shard_map/ppermute | solution.py:251
  13.8 5.5 %collective-permute-start.4 = (bf16[5,64,128]{2,1,0:T(8,128)(2,1)S(1)}, bf16[5,64,128]{2,1,0:T(8,128)(2,1)S(1)}, u32[]{:S(2)}, u32[]{:S(2)}) collective-permute-start(bf16[5,64,128]{2,1,0:T(8,128)(2,1)S(1)} %cross_level.18.after_ref.own_ref), channel_id=1, source_target_pairs={{0,4},{4,0},{8,12},{12,8},{16,20},{20,16},{24,28},{28,24},{1,5},{5... | collective-permute-start | bytes 245768 | tf_op jit(solution)/shard_map/ppermute | solution.py:251
  15.8 3.5 %copy-start = (bf16[64,3,64,128]{3,2,1,0:T(8,128)(2,1)S(1)}, bf16[64,3,64,128]{3,2,1,0:T(8,128)(2,1)}, u32[]{:S(2)}) copy-start(bf16[64,3,64,128]{3,2,1,0:T(8,128)(2,1)} %mix_ref.39) | copy-start | bytes 9437188
  15.8 6.5 %collective-permute-start.7 = (bf16[10,64,128]{2,1,0:T(8,128)(2,1)S(1)}, bf16[10,64,128]{2,1,0:T(8,128)(2,1)S(1)}, u32[]{:S(2)}, u32[]{:S(2)}) collective-permute-start(bf16[10,64,128]{2,1,0:T(8,128)(2,1)S(1)} %cross_level.19.after_ref.own_ref), channel_id=1, source_target_pairs={{0,2},{1,3},{2,0},{3,1},{4,6},{5,7},{6,4},{7,5},{8,10},{9,11},{10,... | collective-permute-start | bytes 491528 | tf_op jit(solution)/shard_map/ppermute | solution.py:251
  17.6 6.4 %collective-permute-start.10 = (bf16[8,64,128]{2,1,0:T(8,128)(2,1)S(1)}, bf16[8,64,128]{2,1,0:T(8,128)(2,1)S(1)}, u32[]{:S(2)}, u32[]{:S(2)}) collective-permute-start(bf16[8,64,128]{2,1,0:T(8,128)(2,1)S(1)} %cross_level.20.after_ref.own_ref), channel_id=1, source_target_pairs={{0,4},{4,0},{8,12},{12,8},{16,20},{20,16},{24,28},{28,24},{1,5},{5... | collective-permute-start | bytes 393224 | tf_op jit(solution)/shard_map/ppermute | solution.py:251
  19.5 5.3 %collective-permute-start.9 = (bf16[5,64,128]{2,1,0:T(8,128)(2,1)S(1)}, bf16[5,64,128]{2,1,0:T(8,128)(2,1)S(1)}, u32[]{:S(2)}, u32[]{:S(2)}) collective-permute-start(bf16[5,64,128]{2,1,0:T(8,128)(2,1)S(1)} %cross_level.21.after_ref.own_ref), channel_id=1, source_target_pairs={{0,8},{4,12},{8,0},{12,4},{16,24},{20,28},{24,16},{28,20},{1,9},{5... | collective-permute-start | bytes 245768 | tf_op jit(solution)/shard_map/ppermute | solution.py:251
  21.4 8.1 %collective-permute-start.6 = (bf16[9,64,128]{2,1,0:T(8,128)(2,1)S(1)}, bf16[9,64,128]{2,1,0:T(8,128)(2,1)S(1)}, u32[]{:S(2)}, u32[]{:S(2)}) collective-permute-start(bf16[9,64,128]{2,1,0:T(8,128)(2,1)S(1)} %cross_level.22.after_ref.own_ref), channel_id=1, source_target_pairs={{0,2},{1,3},{2,0},{3,1},{4,6},{5,7},{6,4},{7,5},{8,10},{9,11},{10,... | collective-permute-start | bytes 442376 | tf_op jit(solution)/shard_map/ppermute | solution.py:251
  22.5 5.4 %collective-permute-start.8 = (bf16[10,64,128]{2,1,0:T(8,128)(2,1)S(1)}, bf16[10,64,128]{2,1,0:T(8,128)(2,1)S(1)}, u32[]{:S(2)}, u32[]{:S(2)}) collective-permute-start(bf16[10,64,128]{2,1,0:T(8,128)(2,1)S(1)} %cross_level.23.after_ref.own_ref), channel_id=1, source_target_pairs={{0,4},{4,0},{8,12},{12,8},{16,20},{20,16},{24,28},{28,24},{1,5},{5... | collective-permute-start | bytes 491528 | tf_op jit(solution)/shard_map/ppermute | solution.py:251
  24.2 6.5 %collective-permute-start.12 = (bf16[8,64,128]{2,1,0:T(8,128)(2,1)S(1)}, bf16[8,64,128]{2,1,0:T(8,128)(2,1)S(1)}, u32[]{:S(2)}, u32[]{:S(2)}) collective-permute-start(bf16[8,64,128]{2,1,0:T(8,128)(2,1)S(1)} %cross_level.24.after_ref.own_ref), channel_id=1, source_target_pairs={{0,8},{4,12},{8,0},{12,4},{16,24},{20,28},{24,16},{28,20},{1,9},{5... | collective-permute-start | bytes 393224 | tf_op jit(solution)/shard_map/ppermute | solution.py:251
  24.9 19.3 %collective-permute-start.18 = (bf16[5,64,128]{2,1,0:T(8,128)(2,1)S(1)}, bf16[5,64,128]{2,1,0:T(8,128)(2,1)S(1)}, u32[]{:S(2)}, u32[]{:S(2)}) collective-permute-start(bf16[5,64,128]{2,1,0:T(8,128)(2,1)S(1)} %cross_level.25.after_ref.own_ref), channel_id=1, source_target_pairs={{0,16},{4,20},{8,24},{12,28},{16,0},{20,4},{24,8},{28,12},{1,17},{... | collective-permute-start | bytes 245768 | tf_op jit(solution)/shard_map/ppermute | solution.py:251
  28.2 8.6 %collective-permute-start.14 = (bf16[10,64,128]{2,1,0:T(8,128)(2,1)S(1)}, bf16[10,64,128]{2,1,0:T(8,128)(2,1)S(1)}, u32[]{:S(2)}, u32[]{:S(2)}) collective-permute-start(bf16[10,64,128]{2,1,0:T(8,128)(2,1)S(1)} %cross_level.26.after_ref.own_ref), channel_id=1, source_target_pairs={{0,8},{4,12},{8,0},{12,4},{16,24},{20,28},{24,16},{28,20},{1,9},{5... | collective-permute-start | bytes 491528 | tf_op jit(solution)/shard_map/ppermute | solution.py:251
  29.7 5.2 %collective-permute-start.11 = (bf16[9,64,128]{2,1,0:T(8,128)(2,1)S(1)}, bf16[9,64,128]{2,1,0:T(8,128)(2,1)S(1)}, u32[]{:S(2)}, u32[]{:S(2)}) collective-permute-start(bf16[9,64,128]{2,1,0:T(8,128)(2,1)S(1)} %cross_level.27.after_ref.own_ref), channel_id=1, source_target_pairs={{0,4},{4,0},{8,12},{12,8},{16,20},{20,16},{24,28},{28,24},{1,5},{5... | collective-permute-start | bytes 442376 | tf_op jit(solution)/shard_map/ppermute | solution.py:251
  31.0 14.4 %collective-permute-start.17 = (bf16[8,64,128]{2,1,0:T(8,128)(2,1)S(1)}, bf16[8,64,128]{2,1,0:T(8,128)(2,1)S(1)}, u32[]{:S(2)}, u32[]{:S(2)}) collective-permute-start(bf16[8,64,128]{2,1,0:T(8,128)(2,1)S(1)} %cross_level.28.after_ref.own_ref), channel_id=1, source_target_pairs={{0,16},{4,20},{8,24},{12,28},{16,0},{20,4},{24,8},{28,12},{1,17},{... | collective-permute-start | bytes 393224 | tf_op jit(solution)/shard_map/ppermute | solution.py:251
  35.2 6.4 %collective-permute-start.13 = (bf16[9,64,128]{2,1,0:T(8,128)(2,1)S(1)}, bf16[9,64,128]{2,1,0:T(8,128)(2,1)S(1)}, u32[]{:S(2)}, u32[]{:S(2)}) collective-permute-start(bf16[9,64,128]{2,1,0:T(8,128)(2,1)S(1)} %cross_level.29.after_ref.own_ref), channel_id=1, source_target_pairs={{0,8},{4,12},{8,0},{12,4},{16,24},{20,28},{24,16},{28,20},{1,9},{5... | collective-permute-start | bytes 442376 | tf_op jit(solution)/shard_map/ppermute | solution.py:251
  37.1 7.2 %copy-start.2 = (bf16[64,64,256]{2,1,0:T(8,128)(2,1)S(1)}, bf16[64,64,256]{2,1,0:T(8,128)(2,1)}, u32[]{:S(2)}) copy-start(bf16[64,64,256]{2,1,0:T(8,128)(2,1)} %leaf_ref.7) | copy-start | bytes 6291460
  37.1 13.5 %collective-permute-start.16 = (bf16[10,64,128]{2,1,0:T(8,128)(2,1)S(1)}, bf16[10,64,128]{2,1,0:T(8,128)(2,1)S(1)}, u32[]{:S(2)}, u32[]{:S(2)}) collective-permute-start(bf16[10,64,128]{2,1,0:T(8,128)(2,1)S(1)} %cross_level.30.after_ref.own_ref), channel_id=1, source_target_pairs={{0,16},{4,20},{8,24},{12,28},{16,0},{20,4},{24,8},{28,12},{1,17},{... | collective-permute-start | bytes 491528 | tf_op jit(solution)/shard_map/ppermute | solution.py:251
  41.8 10.5 %collective-permute-start.15 = (bf16[9,64,128]{2,1,0:T(8,128)(2,1)S(1)}, bf16[9,64,128]{2,1,0:T(8,128)(2,1)S(1)}, u32[]{:S(2)}, u32[]{:S(2)}) collective-permute-start(bf16[9,64,128]{2,1,0:T(8,128)(2,1)S(1)} %cross_level.31.rest_0_.own_ref), channel_id=1, source_target_pairs={{0,16},{4,20},{8,24},{12,28},{16,0},{20,4},{24,8},{28,12},{1,17},{... | collective-permute-start | bytes 442376 | tf_op jit(solution)/shard_map/ppermute | solution.py:251

commit v3 on v1

--- a/solution.py
+++ b/solution.py
@@ -9,7 +9,7 @@
 
 NT = (((1,), (1,)), ((), ()))
 PIECES = 4
-SHARES = (5, 9, 10, 8)
+SHARES = (5, 8, 10, 9)
 LAGS = (
     (1.0, 1.1, 1.2, 1.3),
     (0.0, 0.5, 1.2, 1.6),
@@ -48,7 +48,7 @@
     first,
     state,
     last_mix,
-    lo_mix,
+    lo_head,
     even,
     odd,
     src,
@@ -77,11 +77,12 @@
         held = mix.at[level] if level < levels - 1 else last_mix
         return pltpu.make_async_copy(mix_hbm.at[:, level], held, mix_sem.at[level])
 
-    next_levels = pltpu.make_async_copy(lo_hbm, lo_mix, lo_sem)
     for piece in range(PIECES):
         for copy in inputs(piece):
             copy.start()
 
+    head = pl.ds(0, lo_head.shape[0])
+    next_level = pltpu.make_async_copy(lo_hbm.at[head, pl.ds(0, 1)], lo_head, lo_sem)
     queue = [factors(level) for level in range(levels)]
     for piece in range(PIECES):
         for copy in inputs(piece):
@@ -97,7 +98,8 @@
                 preferred_element_type=jnp.float32,
             )
             even[pair] = pack(product).astype(even.dtype)
-    next_levels.start()
+
+    next_level.start()
 
     for level in range(levels):
         factors(level).wait()
@@ -112,10 +114,10 @@
             chosen = last_mix if level == levels - 1 else mix.at[level]
             part = chosen[2 * pair : 2 * pair + 2]
             new[pair] = mix_pair(own, other, part).astype(own.dtype)
-    next_levels.wait()
-
-
-def local_phase(sources, leaf_in, local_mix, lo_mix, size):
+    next_level.wait()
+
+
+def local_phase(sources, leaf_in, local_mix, lo_mix, size, blocks_next):
     vectors = sources.shape[0]
     blocks, rank, _ = leaf_in.shape
     levels = local_mix.shape[1]
@@ -125,7 +127,7 @@
             pltpu.VMEM((size, rank, 2 * vectors), jnp.bfloat16),
             pltpu.VMEM((blocks // 2, rank, 2 * vectors), jnp.bfloat16),
             pltpu.VMEM((blocks,) + local_mix.shape[2:], local_mix.dtype),
-            pltpu.VMEM(lo_mix.shape, lo_mix.dtype),
+            pltpu.VMEM((blocks_next, 1) + lo_mix.shape[2:], lo_mix.dtype),
         ],
         in_specs=[pl.BlockSpec(memory_space=pltpu.HBM)] * 4,
         out_specs=[pl.BlockSpec(memory_space=pltpu.VMEM)] * 4,
@@ -280,8 +282,9 @@
         lags = LAGS[min(end - s, 3) if s else 4]
         return s + lags[c], -s
 
-    first, state, last_mix, lo_mix = local_phase(sources, leaf_in, local_mix, lo_mix, head)
-    steps[:lo_levels] = [("lo", n, lo_mix) for n in range(lo_levels)]
+    first, state, last_mix, lo_head = local_phase(
+        sources, leaf_in, local_mix, lo_mix, head, 2 * parts[1][1]
+    )
     axis, level, _ = steps[0]
     waiting[0, 0] = first, swapped(first, axis, level), 0
     after = state
@@ -289,6 +292,8 @@
     for s, c in sorted(((s, c) for s in range(end + 1) for c in range(len(parts))), key=turn):
         own, other, offset = waiting.pop((s, c))
         _, level, mix = steps[s]
+        if s == 0 and c < 2:
+            mix = lo_head
         start, stop = parts[c]
         if s == end:
             more = c < len(parts) - 1

time: 53.7 us -> 53.3 us (level)
  transfers between devices with their start and end apart: 19 -> 19, of which waited for: 10 -> 9; matrix products, arithmetic and copies ran while one was open for 0% -> 0% of each run, Pallas kernels for 14% -> 14%
where the time goes in v3:
time: 53.3 us; the launch traced here: 53.2 us
  starting transfers between devices  26.7 us (50%)
  Pallas kernels  14.2 us (27%)
  waiting for transfers between devices  12 us (23%)
    ppermute x19, starting transfers between devices, swapped(): return lax.ppermute(block, axis, route)  26.7 us
    ppermute x19, waiting for transfers between devices, swapped(): return lax.ppermute(block, axis, route)  12 us
    pallas_call x1, Pallas kernels, local_phase(): pl.pallas_call(local_kernel, out_shape=[pltpu.VMEM((size, rank, 2 * vecto...  5.25 us
    pallas_call x4, Pallas kernels, final_level(): pl.pallas_call(functools.partial(final_kernel, has_token, level, start),...  4.96 us
    pallas_call x16, Pallas kernels, cross_level(): pl.pallas_call(functools.partial(cross_kernel, level, start, offset), out...  3.46 us
  transfers between devices with their start and end apart: 19, of which 9 were waited for; matrix products, arithmetic and copies ran while one was open for 0% of the time, Pallas kernels for 14%

profile of v3, /device:TPU:0, one launch (start us, length us, event | category | flops | bytes accessed | tf_op | source)
XLA Modules:
  0.0 53.2 jit_solution(8511794884432426267)
XLA Ops:
  0.0 5.3 %local_levels.1 = (bf16[5,64,128]{2,1,0:T(8,128)(2,1)S(1)}, bf16[32,64,128]{2,1,0:T(8,128)(2,1)S(1)}, bf16[64,64,128]{2,1,0:T(8,128)(2,1)S(1)}, bf16[26,1,64,128]{3,2,1,0:T(8,128)(2,1)S(1)}) custom-call(bf16[64,16384]{1,0:T(8,128)(2,1)} %src_hbm.1, bf16[64,64,256]{2,1,0:T(8,128)(2,1)} %leaf_hbm.1, bf16[64,6,64,128]{3,2,1,0:T(8,128)(2,1)} %mix_hbm.1, ...), custom_call_target="tpu_custom_call" | custom-call | flops 1000000000 | bytes 10485760 | tf_op jit(solution)/shard_map/local_levels/pallas_call | solution.py:124
  5.3 0.5 collective-permute-start
  5.8 0.9 %collective-permute-done.other_ref = bf16[5,64,128]{2,1,0:T(8,128)(2,1)S(1)} collective-permute-done((bf16[5,64,128]{2,1,0:T(8,128)(2,1)S(1)}, bf16[5,64,128]{2,1,0:T(8,128)(2,1)S(1)}, u32[]{:S(2)}, u32[]{:S(2)}) %collective-permute-start) | collective-permute-done | bytes 81952 | tf_op jit(solution)/shard_map/ppermute | solution.py:261
  6.9 0.2 local_rest.2.own_ref.after_ref
  7.1 0.4 collective-permute-start.1
  7.5 2.7 %collective-permute-start.3 = (bf16[5,64,128]{2,1,0:T(8,128)(2,1)S(1)}, bf16[5,64,128]{2,1,0:T(8,128)(2,1)S(1)}, u32[]{:S(2)}, u32[]{:S(2)}) collective-permute-start(bf16[5,64,128]{2,1,0:T(8,128)(2,1)S(1)} %cross_level.16.after_ref.own_ref), channel_id=1, source_target_pairs={{0,2},{1,3},{2,0},{3,1},{4,6},{5,7},{6,4},{7,5},{8,10},{9,11},{10,... | collective-permute-start | bytes 245768 | tf_op jit(solution)/shard_map/ppermute | solution.py:261
  10.2 0.2 cross_level.17.after_ref.own_ref
  10.4 0.3 local_rest.3.after_ref.own_ref
  10.9 1.3 %collective-permute-start.5 = (bf16[8,64,128]{2,1,0:T(8,128)(2,1)S(1)}, bf16[8,64,128]{2,1,0:T(8,128)(2,1)S(1)}, u32[]{:S(2)}, u32[]{:S(2)}) collective-permute-start(bf16[8,64,128]{2,1,0:T(8,128)(2,1)S(1)} %cross_level.17.after_ref.own_ref), channel_id=1, source_target_pairs={{0,2},{1,3},{2,0},{3,1},{4,6},{5,7},{6,4},{7,5},{8,10},{9,11},{10,... | collective-permute-start | bytes 393224 | tf_op jit(solution)/shard_map/ppermute | solution.py:261
  12.2 1.0 %collective-permute-done.3.other_ref = bf16[5,64,128]{2,1,0:T(8,128)(2,1)S(1)} collective-permute-done((bf16[5,64,128]{2,1,0:T(8,128)(2,1)S(1)}, bf16[5,64,128]{2,1,0:T(8,128)(2,1)S(1)}, u32[]{:S(2)}, u32[]{:S(2)}) %collective-permute-start.3) | collective-permute-done | bytes 81952 | tf_op jit(solution)/shard_map/ppermute | solution.py:261
  13.2 0.2 cross_level.18.after_ref.own_ref
  13.4 1.8 %collective-permute-start.4 = (bf16[5,64,128]{2,1,0:T(8,128)(2,1)S(1)}, bf16[5,64,128]{2,1,0:T(8,128)(2,1)S(1)}, u32[]{:S(2)}, u32[]{:S(2)}) collective-permute-start(bf16[5,64,128]{2,1,0:T(8,128)(2,1)S(1)} %cross_level.18.after_ref.own_ref), channel_id=1, source_target_pairs={{0,4},{4,0},{8,12},{12,8},{16,20},{20,16},{24,28},{28,24},{1,5},{5... | collective-permute-start | bytes 245768 | tf_op jit(solution)/shard_map/ppermute | solution.py:261
  15.1 0.2 cross_level.19.after_ref.own_ref
  15.4 1.6 %collective-permute-start.7 = (bf16[10,64,128]{2,1,0:T(8,128)(2,1)S(1)}, bf16[10,64,128]{2,1,0:T(8,128)(2,1)S(1)}, u32[]{:S(2)}, u32[]{:S(2)}) collective-permute-start(bf16[10,64,128]{2,1,0:T(8,128)(2,1)S(1)} %cross_level.19.after_ref.own_ref), channel_id=1, source_target_pairs={{0,2},{1,3},{2,0},{3,1},{4,6},{5,7},{6,4},{7,5},{8,10},{9,11},{10,... | collective-permute-start | bytes 491528 | tf_op jit(solution)/shard_map/ppermute | solution.py:261
  17.0 0.2 cross_level.20.after_ref.own_ref
  17.2 1.7 %collective-permute-start.10 = (bf16[8,64,128]{2,1,0:T(8,128)(2,1)S(1)}, bf16[8,64,128]{2,1,0:T(8,128)(2,1)S(1)}, u32[]{:S(2)}, u32[]{:S(2)}) collective-permute-start(bf16[8,64,128]{2,1,0:T(8,128)(2,1)S(1)} %cross_level.20.after_ref.own_ref), channel_id=1, source_target_pairs={{0,4},{4,0},{8,12},{12,8},{16,20},{20,16},{24,28},{28,24},{1,5},{5... | collective-permute-start | bytes 393224 | tf_op jit(solution)/shard_map/ppermute | solution.py:261
  18.9 0.2 cross_level.21.after_ref.own_ref
  19.1 1.6 %collective-permute-start.9 = (bf16[5,64,128]{2,1,0:T(8,128)(2,1)S(1)}, bf16[5,64,128]{2,1,0:T(8,128)(2,1)S(1)}, u32[]{:S(2)}, u32[]{:S(2)}) collective-permute-start(bf16[5,64,128]{2,1,0:T(8,128)(2,1)S(1)} %cross_level.21.after_ref.own_ref), channel_id=1, source_target_pairs={{0,8},{4,12},{8,0},{12,4},{16,24},{20,28},{24,16},{28,20},{1,9},{5... | collective-permute-start | bytes 245768 | tf_op jit(solution)/shard_map/ppermute | solution.py:261
  20.7 0.2 cross_level.22.after_ref.own_ref
  20.9 0.9 %collective-permute-start.6 = (bf16[9,64,128]{2,1,0:T(8,128)(2,1)S(1)}, bf16[9,64,128]{2,1,0:T(8,128)(2,1)S(1)}, u32[]{:S(2)}, u32[]{:S(2)}) collective-permute-start(bf16[9,64,128]{2,1,0:T(8,128)(2,1)S(1)} %cross_level.22.after_ref.own_ref), channel_id=1, source_target_pairs={{0,2},{1,3},{2,0},{3,1},{4,6},{5,7},{6,4},{7,5},{8,10},{9,11},{10,... | collective-permute-start | bytes 442376 | tf_op jit(solution)/shard_map/ppermute | solution.py:261
  21.9 0.2 cross_level.23.after_ref.own_ref
  22.1 1.4 %collective-permute-start.8 = (bf16[10,64,128]{2,1,0:T(8,128)(2,1)S(1)}, bf16[10,64,128]{2,1,0:T(8,128)(2,1)S(1)}, u32[]{:S(2)}, u32[]{:S(2)}) collective-permute-start(bf16[10,64,128]{2,1,0:T(8,128)(2,1)S(1)} %cross_level.23.after_ref.own_ref), channel_id=1, source_target_pairs={{0,4},{4,0},{8,12},{12,8},{16,20},{20,16},{24,28},{28,24},{1,5},{5... | collective-permute-start | bytes 491528 | tf_op jit(solution)/shard_map/ppermute | solution.py:261
  23.6 0.2 cross_level.24.after_ref.own_ref
  23.8 0.5 collective-permute-start.12
  24.5 2.7 %collective-permute-start.18 = (bf16[5,64,128]{2,1,0:T(8,128)(2,1)S(1)}, bf16[5,64,128]{2,1,0:T(8,128)(2,1)S(1)}, u32[]{:S(2)}, u32[]{:S(2)}) collective-permute-start(bf16[5,64,128]{2,1,0:T(8,128)(2,1)S(1)} %cross_level.25.after_ref.own_ref), channel_id=1, source_target_pairs={{0,16},{4,20},{8,24},{12,28},{16,0},{20,4},{24,8},{28,12},{1,17},{... | collective-permute-start | bytes 245768 | tf_op jit(solution)/shard_map/ppermute | solution.py:261
  27.1 0.3 collective-permute-done.8.other_ref
  27.5 0.2 cross_level.26.after_ref.own_ref
  27.7 1.3 %collective-permute-start.14 = (bf16[10,64,128]{2,1,0:T(8,128)(2,1)S(1)}, bf16[10,64,128]{2,1,0:T(8,128)(2,1)S(1)}, u32[]{:S(2)}, u32[]{:S(2)}) collective-permute-start(bf16[10,64,128]{2,1,0:T(8,128)(2,1)S(1)} %cross_level.26.after_ref.own_ref), channel_id=1, source_target_pairs={{0,8},{4,12},{8,0},{12,4},{16,24},{20,28},{24,16},{28,20},{1,9},{5... | collective-permute-start | bytes 491528 | tf_op jit(solution)/shard_map/ppermute | solution.py:261
  29.0 0.2 cross_level.27.after_ref.own_ref
  29.3 0.7 %collective-permute-start.11 = (bf16[9,64,128]{2,1,0:T(8,128)(2,1)S(1)}, bf16[9,64,128]{2,1,0:T(8,128)(2,1)S(1)}, u32[]{:S(2)}, u32[]{:S(2)}) collective-permute-start(bf16[9,64,128]{2,1,0:T(8,128)(2,1)S(1)} %cross_level.27.after_ref.own_ref), channel_id=1, source_target_pairs={{0,4},{4,0},{8,12},{12,8},{16,20},{20,16},{24,28},{28,24},{1,5},{5... | collective-permute-start | bytes 442376 | tf_op jit(solution)/shard_map/ppermute | solution.py:261
  30.0 0.3 collective-permute-done.12.other_ref
  30.3 0.2 cross_level.28.after_ref.own_ref
  30.5 2.3 %collective-permute-start.17 = (bf16[8,64,128]{2,1,0:T(8,128)(2,1)S(1)}, bf16[8,64,128]{2,1,0:T(8,128)(2,1)S(1)}, u32[]{:S(2)}, u32[]{:S(2)}) collective-permute-start(bf16[8,64,128]{2,1,0:T(8,128)(2,1)S(1)} %cross_level.28.after_ref.own_ref), channel_id=1, source_target_pairs={{0,16},{4,20},{8,24},{12,28},{16,0},{20,4},{24,8},{28,12},{1,17},{... | collective-permute-start | bytes 393224 | tf_op jit(solution)/shard_map/ppermute | solution.py:261
  32.8 1.7 %collective-permute-done.11.other_ref = bf16[9,64,128]{2,1,0:T(8,128)(2,1)S(1)} collective-permute-done((bf16[9,64,128]{2,1,0:T(8,128)(2,1)S(1)}, bf16[9,64,128]{2,1,0:T(8,128)(2,1)S(1)}, u32[]{:S(2)}, u32[]{:S(2)}) %collective-permute-start.11) | collective-permute-done | bytes 147488 | tf_op jit(solution)/shard_map/ppermute | solution.py:261
  34.5 0.2 cross_level.29.after_ref.own_ref
  34.7 0.9 %collective-permute-start.13 = (bf16[9,64,128]{2,1,0:T(8,128)(2,1)S(1)}, bf16[9,64,128]{2,1,0:T(8,128)(2,1)S(1)}, u32[]{:S(2)}, u32[]{:S(2)}) collective-permute-start(bf16[9,64,128]{2,1,0:T(8,128)(2,1)S(1)} %cross_level.29.after_ref.own_ref), channel_id=1, source_target_pairs={{0,8},{4,12},{8,0},{12,4},{16,24},{20,28},{24,16},{28,20},{1,9},{5... | collective-permute-start | bytes 442376 | tf_op jit(solution)/shard_map/ppermute | solution.py:261
  35.6 0.8 %collective-permute-done.14.other_ref = bf16[10,64,128]{2,1,0:T(8,128)(2,1)S(1)} collective-permute-done((bf16[10,64,128]{2,1,0:T(8,128)(2,1)S(1)}, bf16[10,64,128]{2,1,0:T(8,128)(2,1)S(1)}, u32[]{:S(2)}, u32[]{:S(2)}) %collective-permute-start.14) | collective-permute-done | bytes 163872 | tf_op jit(solution)/shard_map/ppermute | solution.py:261
  36.4 0.2 cross_level.30.after_ref.own_ref
  36.6 1.9 %collective-permute-start.16 = (bf16[10,64,128]{2,1,0:T(8,128)(2,1)S(1)}, bf16[10,64,128]{2,1,0:T(8,128)(2,1)S(1)}, u32[]{:S(2)}, u32[]{:S(2)}) collective-permute-start(bf16[10,64,128]{2,1,0:T(8,128)(2,1)S(1)} %cross_level.30.after_ref.own_ref), channel_id=1, source_target_pairs={{0,16},{4,20},{8,24},{12,28},{16,0},{20,4},{24,8},{28,12},{1,17},{... | collective-permute-start | bytes 491528 | tf_op jit(solution)/shard_map/ppermute | solution.py:261
  38.5 2.6 %collective-permute-done.13.other_ref = bf16[9,64,128]{2,1,0:T(8,128)(2,1)S(1)} collective-permute-done((bf16[9,64,128]{2,1,0:T(8,128)(2,1)S(1)}, bf16[9,64,128]{2,1,0:T(8,128)(2,1)S(1)}, u32[]{:S(2)}, u32[]{:S(2)}) %collective-permute-start.13) | collective-permute-done | bytes 147488 | tf_op jit(solution)/shard_map/ppermute | solution.py:261
  41.1 0.2 cross_level.31.rest_0_.own_ref
  41.3 2.5 %collective-permute-start.15 = (bf16[9,64,128]{2,1,0:T(8,128)(2,1)S(1)}, bf16[9,64,128]{2,1,0:T(8,128)(2,1)S(1)}, u32[]{:S(2)}, u32[]{:S(2)}) collective-permute-start(bf16[9,64,128]{2,1,0:T(8,128)(2,1)S(1)} %cross_level.31.rest_0_.own_ref), channel_id=1, source_target_pairs={{0,16},{4,20},{8,24},{12,28},{16,0},{20,4},{24,8},{28,12},{1,17},{... | collective-permute-start | bytes 442376 | tf_op jit(solution)/shard_map/ppermute | solution.py:261
  43.8 1.1 %final_level.4 = (bf16[64,16384]{1,0:T(8,128)(2,1)}, f32[8,128]{1,0:T(8,128)S(1)}) custom-call(bf16[5,64,128]{2,1,0:T(8,128)(2,1)S(1)} %cross_level.25.after_ref.own_ref, bf16[5,64,128]{2,1,0:T(8,128)(2,1)S(1)} %collective-permute-done.18.other_ref, bf16[64,3,64,128]{3,2,1,0:T(8,128)(2,1)S(1)} %copy-done.1, bf16[64,64,256]{2,1,0:T(8,128)(2,1)S(1)} %copy-done.2, ...), custom_call_target="tpu_custom_call" | custom-call | flops 3000000000 | tf_op jit(solution)/shard_map/final_level/pallas_call | solution.py:240
  45.0 1.2 %final_level.5 = (bf16[64,16384]{1,0:T(8,128)(2,1)}, f32[8,128]{1,0:T(8,128)S(1)}) custom-call(bf16[8,64,128]{2,1,0:T(8,128)(2,1)S(1)} %cross_level.28.after_ref.own_ref, bf16[8,64,128]{2,1,0:T(8,128)(2,1)S(1)} %collective-permute-done.17.other_ref, bf16[64,3,64,128]{3,2,1,0:T(8,128)(2,1)S(1)} %copy-done.1, ...), custom_call_target="tpu_custom_call", output_to_operand_aliasing={{0}: (5, {})} | custom-call | flops 3000000000 | tf_op jit(solution)/shard_map/final_level/pallas_call | solution.py:240
  46.2 3.9 %collective-permute-done.16.other_ref = bf16[10,64,128]{2,1,0:T(8,128)(2,1)S(1)} collective-permute-done((bf16[10,64,128]{2,1,0:T(8,128)(2,1)S(1)}, bf16[10,64,128]{2,1,0:T(8,128)(2,1)S(1)}, u32[]{:S(2)}, u32[]{:S(2)}) %collective-permute-start.16) | collective-permute-done | bytes 163872 | tf_op jit(solution)/shard_map/ppermute | solution.py:261
  50.1 1.3 %final_level.6 = (bf16[64,16384]{1,0:T(8,128)(2,1)}, f32[8,128]{1,0:T(8,128)S(1)}) custom-call(bf16[10,64,128]{2,1,0:T(8,128)(2,1)S(1)} %cross_level.30.after_ref.own_ref, bf16[10,64,128]{2,1,0:T(8,128)(2,1)S(1)} %collective-permute-done.16.other_ref, bf16[64,3,64,128]{3,2,1,0:T(8,128)(2,1)S(1)} %copy-done.1, ...), custom_call_target="tpu_custom_call", output_to_operand_aliasing={{0}: (5, {})} | custom-call | flops 3000000000 | tf_op jit(solution)/shard_map/final_level/pallas_call | solution.py:240
  51.5 0.4 collective-permute-done.15.other_ref
  51.9 1.3 %final_level.7 = bf16[64,16384]{1,0:T(8,128)(2,1)} custom-call(bf16[9,64,128]{2,1,0:T(8,128)(2,1)S(1)} %cross_level.31.rest_0_.own_ref, bf16[9,64,128]{2,1,0:T(8,128)(2,1)S(1)} %collective-permute-done.15.other_ref, bf16[64,3,64,128]{3,2,1,0:T(8,128)(2,1)S(1)} %copy-done.1, bf16[64,64,256]{2,1,0:T(8,128)(2,1)S(1)} %copy-done.2, ...), custom_call_target="tpu_custom_call", output_to_operand_aliasing={{}: (5, {})} | custom-call | flops 3000000000 | tf_op jit(solution)/shard_map/final_level/pallas_call | solution.py:240
  (19 shorter events, 0.6 us)
Async XLA Ops:
  5.3 1.4 %collective-permute-start = (bf16[5,64,128]{2,1,0:T(8,128)(2,1)S(1)}, bf16[5,64,128]{2,1,0:T(8,128)(2,1)S(1)}, u32[]{:S(2)}, u32[]{:S(2)}) collective-permute-start(bf16[5,64,128]{2,1,0:T(8,128)(2,1)S(1)} %get-tuple-element.17.own_ref), channel_id=1, source_target_pairs={{0,1},{1,0},{2,3},{3,2},{4,5},{5,4},{6,7},{7,6},{8,9},{9,8},{10,11... | collective-permute-start | bytes 245768 | tf_op jit(solution)/shard_map/ppermute | solution.py:261
  7.1 3.1 %collective-permute-start.1 = (bf16[8,64,128]{2,1,0:T(8,128)(2,1)S(1)}, bf16[8,64,128]{2,1,0:T(8,128)(2,1)S(1)}, u32[]{:S(2)}, u32[]{:S(2)}) collective-permute-start(bf16[8,64,128]{2,1,0:T(8,128)(2,1)S(1)} %local_rest.2.own_ref.after_ref), channel_id=1, source_target_pairs={{0,1},{1,0},{2,3},{3,2},{4,5},{5,4},{6,7},{7,6},{8,9},{9,8},{10,11... | collective-permute-start | bytes 393224 | tf_op jit(solution)/shard_map/ppermute | solution.py:261
  7.5 5.6 %collective-permute-start.3 = (bf16[5,64,128]{2,1,0:T(8,128)(2,1)S(1)}, bf16[5,64,128]{2,1,0:T(8,128)(2,1)S(1)}, u32[]{:S(2)}, u32[]{:S(2)}) collective-permute-start(bf16[5,64,128]{2,1,0:T(8,128)(2,1)S(1)} %cross_level.16.after_ref.own_ref), channel_id=1, source_target_pairs={{0,2},{1,3},{2,0},{3,1},{4,6},{5,7},{6,4},{7,5},{8,10},{9,11},{10,... | collective-permute-start | bytes 245768 | tf_op jit(solution)/shard_map/ppermute | solution.py:261
  10.4 2.7 %copy-start = (bf16[64,2,64,128]{3,2,1,0:T(8,128)(2,1)S(1)}, bf16[64,2,64,128]{3,2,1,0:T(8,128)(2,1)}, u32[]{:S(2)}) copy-start(bf16[64,2,64,128]{3,2,1,0:T(8,128)(2,1)} %mix_ref.27) | copy-start | bytes 6291460
  10.8 4.4 %collective-permute-start.2 = (bf16[19,64,128]{2,1,0:T(8,128)(2,1)S(1)}, bf16[19,64,128]{2,1,0:T(8,128)(2,1)S(1)}, u32[]{:S(2)}, u32[]{:S(2)}) collective-permute-start(bf16[19,64,128]{2,1,0:T(8,128)(2,1)S(1)} %local_rest.3.after_ref.own_ref), channel_id=1, source_target_pairs={{0,1},{1,0},{2,3},{3,2},{4,5},{5,4},{6,7},{7,6},{8,9},{9,8},{10,11... | collective-permute-start | bytes 933896 | tf_op jit(solution)/shard_map/ppermute | solution.py:261
  10.9 6.1 %collective-permute-start.5 = (bf16[8,64,128]{2,1,0:T(8,128)(2,1)S(1)}, bf16[8,64,128]{2,1,0:T(8,128)(2,1)S(1)}, u32[]{:S(2)}, u32[]{:S(2)}) collective-permute-start(bf16[8,64,128]{2,1,0:T(8,128)(2,1)S(1)} %cross_level.17.after_ref.own_ref), channel_id=1, source_target_pairs={{0,2},{1,3},{2,0},{3,1},{4,6},{5,7},{6,4},{7,5},{8,10},{9,11},{10,... | collective-permute-start | bytes 393224 | tf_op jit(solution)/shard_map/ppermute | solution.py:261
  13.4 5.5 %collective-permute-start.4 = (bf16[5,64,128]{2,1,0:T(8,128)(2,1)S(1)}, bf16[5,64,128]{2,1,0:T(8,128)(2,1)S(1)}, u32[]{:S(2)}, u32[]{:S(2)}) collective-permute-start(bf16[5,64,128]{2,1,0:T(8,128)(2,1)S(1)} %cross_level.18.after_ref.own_ref), channel_id=1, source_target_pairs={{0,4},{4,0},{8,12},{12,8},{16,20},{20,16},{24,28},{28,24},{1,5},{5... | collective-permute-start | bytes 245768 | tf_op jit(solution)/shard_map/ppermute | solution.py:261
  15.4 3.5 %copy-start.1 = (bf16[64,3,64,128]{3,2,1,0:T(8,128)(2,1)S(1)}, bf16[64,3,64,128]{3,2,1,0:T(8,128)(2,1)}, u32[]{:S(2)}) copy-start(bf16[64,3,64,128]{3,2,1,0:T(8,128)(2,1)} %mix_ref.35) | copy-start | bytes 9437188
  15.4 6.5 %collective-permute-start.7 = (bf16[10,64,128]{2,1,0:T(8,128)(2,1)S(1)}, bf16[10,64,128]{2,1,0:T(8,128)(2,1)S(1)}, u32[]{:S(2)}, u32[]{:S(2)}) collective-permute-start(bf16[10,64,128]{2,1,0:T(8,128)(2,1)S(1)} %cross_level.19.after_ref.own_ref), channel_id=1, source_target_pairs={{0,2},{1,3},{2,0},{3,1},{4,6},{5,7},{6,4},{7,5},{8,10},{9,11},{10,... | collective-permute-start | bytes 491528 | tf_op jit(solution)/shard_map/ppermute | solution.py:261
  17.2 6.3 %collective-permute-start.10 = (bf16[8,64,128]{2,1,0:T(8,128)(2,1)S(1)}, bf16[8,64,128]{2,1,0:T(8,128)(2,1)S(1)}, u32[]{:S(2)}, u32[]{:S(2)}) collective-permute-start(bf16[8,64,128]{2,1,0:T(8,128)(2,1)S(1)} %cross_level.20.after_ref.own_ref), channel_id=1, source_target_pairs={{0,4},{4,0},{8,12},{12,8},{16,20},{20,16},{24,28},{28,24},{1,5},{5... | collective-permute-start | bytes 393224 | tf_op jit(solution)/shard_map/ppermute | solution.py:261
  19.1 5.2 %collective-permute-start.9 = (bf16[5,64,128]{2,1,0:T(8,128)(2,1)S(1)}, bf16[5,64,128]{2,1,0:T(8,128)(2,1)S(1)}, u32[]{:S(2)}, u32[]{:S(2)}) collective-permute-start(bf16[5,64,128]{2,1,0:T(8,128)(2,1)S(1)} %cross_level.21.after_ref.own_ref), channel_id=1, source_target_pairs={{0,8},{4,12},{8,0},{12,4},{16,24},{20,28},{24,16},{28,20},{1,9},{5... | collective-permute-start | bytes 245768 | tf_op jit(solution)/shard_map/ppermute | solution.py:261
  20.9 8.1 %collective-permute-start.6 = (bf16[9,64,128]{2,1,0:T(8,128)(2,1)S(1)}, bf16[9,64,128]{2,1,0:T(8,128)(2,1)S(1)}, u32[]{:S(2)}, u32[]{:S(2)}) collective-permute-start(bf16[9,64,128]{2,1,0:T(8,128)(2,1)S(1)} %cross_level.22.after_ref.own_ref), channel_id=1, source_target_pairs={{0,2},{1,3},{2,0},{3,1},{4,6},{5,7},{6,4},{7,5},{8,10},{9,11},{10,... | collective-permute-start | bytes 442376 | tf_op jit(solution)/shard_map/ppermute | solution.py:261
  22.1 5.4 %collective-permute-start.8 = (bf16[10,64,128]{2,1,0:T(8,128)(2,1)S(1)}, bf16[10,64,128]{2,1,0:T(8,128)(2,1)S(1)}, u32[]{:S(2)}, u32[]{:S(2)}) collective-permute-start(bf16[10,64,128]{2,1,0:T(8,128)(2,1)S(1)} %cross_level.23.after_ref.own_ref), channel_id=1, source_target_pairs={{0,4},{4,0},{8,12},{12,8},{16,20},{20,16},{24,28},{28,24},{1,5},{5... | collective-permute-start | bytes 491528 | tf_op jit(solution)/shard_map/ppermute | solution.py:261
  23.8 6.5 %collective-permute-start.12 = (bf16[8,64,128]{2,1,0:T(8,128)(2,1)S(1)}, bf16[8,64,128]{2,1,0:T(8,128)(2,1)S(1)}, u32[]{:S(2)}, u32[]{:S(2)}) collective-permute-start(bf16[8,64,128]{2,1,0:T(8,128)(2,1)S(1)} %cross_level.24.after_ref.own_ref), channel_id=1, source_target_pairs={{0,8},{4,12},{8,0},{12,4},{16,24},{20,28},{24,16},{28,20},{1,9},{5... | collective-permute-start | bytes 393224 | tf_op jit(solution)/shard_map/ppermute | solution.py:261
  24.5 19.3 %collective-permute-start.18 = (bf16[5,64,128]{2,1,0:T(8,128)(2,1)S(1)}, bf16[5,64,128]{2,1,0:T(8,128)(2,1)S(1)}, u32[]{:S(2)}, u32[]{:S(2)}) collective-permute-start(bf16[5,64,128]{2,1,0:T(8,128)(2,1)S(1)} %cross_level.25.after_ref.own_ref), channel_id=1, source_target_pairs={{0,16},{4,20},{8,24},{12,28},{16,0},{20,4},{24,8},{28,12},{1,17},{... | collective-permute-start | bytes 245768 | tf_op jit(solution)/shard_map/ppermute | solution.py:261
  27.7 8.7 %collective-permute-start.14 = (bf16[10,64,128]{2,1,0:T(8,128)(2,1)S(1)}, bf16[10,64,128]{2,1,0:T(8,128)(2,1)S(1)}, u32[]{:S(2)}, u32[]{:S(2)}) collective-permute-start(bf16[10,64,128]{2,1,0:T(8,128)(2,1)S(1)} %cross_level.26.after_ref.own_ref), channel_id=1, source_target_pairs={{0,8},{4,12},{8,0},{12,4},{16,24},{20,28},{24,16},{28,20},{1,9},{5... | collective-permute-start | bytes 491528 | tf_op jit(solution)/shard_map/ppermute | solution.py:261
  29.3 5.2 %collective-permute-start.11 = (bf16[9,64,128]{2,1,0:T(8,128)(2,1)S(1)}, bf16[9,64,128]{2,1,0:T(8,128)(2,1)S(1)}, u32[]{:S(2)}, u32[]{:S(2)}) collective-permute-start(bf16[9,64,128]{2,1,0:T(8,128)(2,1)S(1)} %cross_level.27.after_ref.own_ref), channel_id=1, source_target_pairs={{0,4},{4,0},{8,12},{12,8},{16,20},{20,16},{24,28},{28,24},{1,5},{5... | collective-permute-start | bytes 442376 | tf_op jit(solution)/shard_map/ppermute | solution.py:261
  30.5 14.5 %collective-permute-start.17 = (bf16[8,64,128]{2,1,0:T(8,128)(2,1)S(1)}, bf16[8,64,128]{2,1,0:T(8,128)(2,1)S(1)}, u32[]{:S(2)}, u32[]{:S(2)}) collective-permute-start(bf16[8,64,128]{2,1,0:T(8,128)(2,1)S(1)} %cross_level.28.after_ref.own_ref), channel_id=1, source_target_pairs={{0,16},{4,20},{8,24},{12,28},{16,0},{20,4},{24,8},{28,12},{1,17},{... | collective-permute-start | bytes 393224 | tf_op jit(solution)/shard_map/ppermute | solution.py:261
  34.7 6.4 %collective-permute-start.13 = (bf16[9,64,128]{2,1,0:T(8,128)(2,1)S(1)}, bf16[9,64,128]{2,1,0:T(8,128)(2,1)S(1)}, u32[]{:S(2)}, u32[]{:S(2)}) collective-permute-start(bf16[9,64,128]{2,1,0:T(8,128)(2,1)S(1)} %cross_level.29.after_ref.own_ref), channel_id=1, source_target_pairs={{0,8},{4,12},{8,0},{12,4},{16,24},{20,28},{24,16},{28,20},{1,9},{5... | collective-permute-start | bytes 442376 | tf_op jit(solution)/shard_map/ppermute | solution.py:261
  36.6 7.2 %copy-start.2 = (bf16[64,64,256]{2,1,0:T(8,128)(2,1)S(1)}, bf16[64,64,256]{2,1,0:T(8,128)(2,1)}, u32[]{:S(2)}) copy-start(bf16[64,64,256]{2,1,0:T(8,128)(2,1)} %leaf_ref.7) | copy-start | bytes 6291460
  36.6 13.5 %collective-permute-start.16 = (bf16[10,64,128]{2,1,0:T(8,128)(2,1)S(1)}, bf16[10,64,128]{2,1,0:T(8,128)(2,1)S(1)}, u32[]{:S(2)}, u32[]{:S(2)}) collective-permute-start(bf16[10,64,128]{2,1,0:T(8,128)(2,1)S(1)} %cross_level.30.after_ref.own_ref), channel_id=1, source_target_pairs={{0,16},{4,20},{8,24},{12,28},{16,0},{20,4},{24,8},{28,12},{1,17},{... | collective-permute-start | bytes 491528 | tf_op jit(solution)/shard_map/ppermute | solution.py:261
  41.3 10.6 %collective-permute-start.15 = (bf16[9,64,128]{2,1,0:T(8,128)(2,1)S(1)}, bf16[9,64,128]{2,1,0:T(8,128)(2,1)S(1)}, u32[]{:S(2)}, u32[]{:S(2)}) collective-permute-start(bf16[9,64,128]{2,1,0:T(8,128)(2,1)S(1)} %cross_level.31.rest_0_.own_ref), channel_id=1, source_target_pairs={{0,16},{4,20},{8,24},{12,28},{16,0},{20,4},{24,8},{28,12},{1,17},{... | collective-permute-start | bytes 442376 | tf_op jit(solution)/shard_map/ppermute | solution.py:261

commit v4 on v3

--- a/solution.py
+++ b/solution.py
@@ -9,7 +9,7 @@
 
 NT = (((1,), (1,)), ((), ()))
 PIECES = 4
-SHARES = (5, 8, 10, 9)
+SHARES = (4, 9, 10, 9)
 LAGS = (
     (1.0, 1.1, 1.2, 1.3),
     (0.0, 0.5, 1.2, 1.6),
@@ -46,6 +46,7 @@
     mix_hbm,
     lo_hbm,
     first,
+    second,
     state,
     last_mix,
     lo_head,
@@ -106,31 +107,39 @@
         old, new = (odd, even) if level % 2 else (even, odd)
         if level == levels - 2:
             new = state
+        count = pairs
         if level == levels - 1:
-            old, new = state, first
-        for pair in range(new.shape[0]):
+            old = state
+            count = first.shape[0] + second.shape[0]
+        for pair in range(count):
             own = old[pair]
             other = half_swap(own) if level == 0 else old[pair ^ 1 << level - 1]
             chosen = last_mix if level == levels - 1 else mix.at[level]
             part = chosen[2 * pair : 2 * pair + 2]
-            new[pair] = mix_pair(own, other, part).astype(own.dtype)
+            mixed = mix_pair(own, other, part).astype(own.dtype)
+            if level < levels - 1:
+                new[pair] = mixed
+            elif pair < first.shape[0]:
+                first[pair] = mixed
+            else:
+                second[pair - first.shape[0]] = mixed
     next_level.wait()
 
 
-def local_phase(sources, leaf_in, local_mix, lo_mix, size, blocks_next):
+def local_phase(sources, leaf_in, local_mix, lo_mix, sizes):
     vectors = sources.shape[0]
     blocks, rank, _ = leaf_in.shape
     levels = local_mix.shape[1]
     return pl.pallas_call(
         local_kernel,
-        out_shape=[
-            pltpu.VMEM((size, rank, 2 * vectors), jnp.bfloat16),
+        out_shape=[pltpu.VMEM((n, rank, 2 * vectors), jnp.bfloat16) for n in sizes]
+        + [
             pltpu.VMEM((blocks // 2, rank, 2 * vectors), jnp.bfloat16),
             pltpu.VMEM((blocks,) + local_mix.shape[2:], local_mix.dtype),
-            pltpu.VMEM((blocks_next, 1) + lo_mix.shape[2:], lo_mix.dtype),
+            pltpu.VMEM((2 * sum(sizes), 1) + lo_mix.shape[2:], lo_mix.dtype),
         ],
         in_specs=[pl.BlockSpec(memory_space=pltpu.HBM)] * 4,
-        out_specs=[pl.BlockSpec(memory_space=pltpu.VMEM)] * 4,
+        out_specs=[pl.BlockSpec(memory_space=pltpu.VMEM)] * 5,
         scratch_shapes=[
             pltpu.VMEM((blocks // 2, rank, 2 * vectors), jnp.bfloat16),
             pltpu.VMEM((blocks // 2, rank, 2 * vectors), jnp.bfloat16),
@@ -274,7 +283,6 @@
     steps += [("hi", n, hi_mix) for n in range(hi_levels)]
     end = len(steps) - 1
     parts = cut(pairs, SHARES)
-    head = parts[0][1]
     waiting = {}
 
     def turn(item):
@@ -282,11 +290,11 @@
         lags = LAGS[min(end - s, 3) if s else 4]
         return s + lags[c], -s
 
-    first, state, last_mix, lo_head = local_phase(
-        sources, leaf_in, local_mix, lo_mix, head, 2 * parts[1][1]
+    *blocks, state, last_mix, lo_head = local_phase(
+        sources, leaf_in, local_mix, lo_mix, [stop - start for start, stop in parts[:2]]
     )
-    axis, level, _ = steps[0]
-    waiting[0, 0] = first, swapped(first, axis, level), 0
+    for c, block in enumerate(blocks):
+        waiting[0, c] = block, swapped(block, *steps[0][:2]), 0
     after = state
     targets = None
     for s, c in sorted(((s, c) for s in range(end + 1) for c in range(len(parts))), key=turn):
@@ -303,9 +311,6 @@
             after = tokens[0] if more else None
             continue
         block = after = cross_level(own, other, mix, level, start, offset, stop - start, after)
-        if s == 0 and c == 0:
-            after = local_rest(state, last_mix, *parts[1], after)
-            waiting[0, 1] = after, swapped(after, *steps[0][:2]), 0
         if s == 0 and c == 1:
             after = rest = local_rest(state, last_mix, stop, pairs, after)
             partner = swapped(rest, *steps[0][:2])

time: 53.3 us -> 53.1 us (level)
  transfers between devices with their start and end apart: 19 -> 19, of which waited for: 9 -> 8; matrix products, arithmetic and copies ran while one was open for 0% -> 0% of each run, Pallas kernels for 14% -> 14%
where the time goes in v4:
time: 53.1 us; the launch traced here: 53 us
  starting transfers between devices  27.1 us (51%)
  Pallas kernels  14.1 us (27%)
  waiting for transfers between devices  11.6 us (22%)
    ppermute x19, starting transfers between devices, swapped(): return lax.ppermute(block, axis, route)  27.1 us
    ppermute x19, waiting for transfers between devices, swapped(): return lax.ppermute(block, axis, route)  11.6 us
    pallas_call x1, Pallas kernels, local_phase(): pl.pallas_call(local_kernel, out_shape=[pltpu.VMEM((n, rank, 2 * vectors)...  5.33 us
    pallas_call x4, Pallas kernels, final_level(): pl.pallas_call(functools.partial(final_kernel, has_token, level, start),...  4.95 us
    pallas_call x16, Pallas kernels, cross_level(): pl.pallas_call(functools.partial(cross_kernel, level, start, offset), out...  3.46 us
  transfers between devices with their start and end apart: 19, of which 8 were waited for; matrix products, arithmetic and copies ran while one was open for 0% of the time, Pallas kernels for 14%

profile of v4, /device:TPU:0, one launch (start us, length us, event | category | flops | bytes accessed | tf_op | source)
XLA Modules:
  0.0 53.0 jit_solution(16268992120243226718)
XLA Ops:
  0.0 5.3 %local_levels.1 = (bf16[4,64,128]{2,1,0:T(8,128)(2,1)S(1)}, bf16[9,64,128]{2,1,0:T(8,128)(2,1)S(1)}, bf16[32,64,128]{2,1,0:T(8,128)(2,1)S(1)}, bf16[64,64,128]{2...) custom-call(bf16[64,16384]{1,0:T(8,128)(2,1)} %src_hbm.1, bf16[64,64,256]{2,1,0:T(8,128)(2,1)} %leaf_hbm.1, ...), custom_call_target="tpu_custom_call" | custom-call | flops 1000000000 | bytes 10485760 | tf_op jit(solution)/shard_map/local_levels/pallas_call | solution.py:133
  5.3 0.5 collective-permute-start.1
  5.9 0.1 collective-permute-start
  5.9 0.8 %collective-permute-done.1.other_ref = bf16[4,64,128]{2,1,0:T(8,128)(2,1)S(1)} collective-permute-done((bf16[4,64,128]{2,1,0:T(8,128)(2,1)S(1)}, bf16[4,64,128]{2,1,0:T(8,128)(2,1)S(1)}, u32[]{:S(2)}, u32[]{:S(2)}) %collective-permute-start.1) | collective-permute-done | bytes 65568 | tf_op jit(solution)/shard_map/ppermute | solution.py:270
  6.8 0.2 cross_level.16.after_ref.own_ref
  6.9 2.9 %collective-permute-start.3 = (bf16[4,64,128]{2,1,0:T(8,128)(2,1)S(1)}, bf16[4,64,128]{2,1,0:T(8,128)(2,1)S(1)}, u32[]{:S(2)}, u32[]{:S(2)}) collective-permute-start(bf16[4,64,128]{2,1,0:T(8,128)(2,1)S(1)} %cross_level.16.after_ref.own_ref), channel_id=1, source_target_pairs={{0,2},{1,3},{2,0},{3,1},{4,6},{5,7},{6,4},{7,5},{8,10},{9,11},{10,... | collective-permute-start | bytes 196616 | tf_op jit(solution)/shard_map/ppermute | solution.py:270
  9.9 0.2 cross_level.17.after_ref.own_ref
  10.1 0.3 local_rest.1.after_ref.own_ref
  10.5 0.4 collective-permute-start.5
  10.9 1.4 %collective-permute-done.3.other_ref = bf16[4,64,128]{2,1,0:T(8,128)(2,1)S(1)} collective-permute-done((bf16[4,64,128]{2,1,0:T(8,128)(2,1)S(1)}, bf16[4,64,128]{2,1,0:T(8,128)(2,1)S(1)}, u32[]{:S(2)}, u32[]{:S(2)}) %collective-permute-start.3) | collective-permute-done | bytes 65568 | tf_op jit(solution)/shard_map/ppermute | solution.py:270
  12.3 0.2 cross_level.18.after_ref.own_ref
  12.5 1.9 %collective-permute-start.4 = (bf16[4,64,128]{2,1,0:T(8,128)(2,1)S(1)}, bf16[4,64,128]{2,1,0:T(8,128)(2,1)S(1)}, u32[]{:S(2)}, u32[]{:S(2)}) collective-permute-start(bf16[4,64,128]{2,1,0:T(8,128)(2,1)S(1)} %cross_level.18.after_ref.own_ref), channel_id=1, source_target_pairs={{0,4},{4,0},{8,12},{12,8},{16,20},{20,16},{24,28},{28,24},{1,5},{5... | collective-permute-start | bytes 196616 | tf_op jit(solution)/shard_map/ppermute | solution.py:270
  14.4 0.2 cross_level.19.after_ref.own_ref
  14.6 1.6 %collective-permute-start.7 = (bf16[10,64,128]{2,1,0:T(8,128)(2,1)S(1)}, bf16[10,64,128]{2,1,0:T(8,128)(2,1)S(1)}, u32[]{:S(2)}, u32[]{:S(2)}) collective-permute-start(bf16[10,64,128]{2,1,0:T(8,128)(2,1)S(1)} %cross_level.19.after_ref.own_ref), channel_id=1, source_target_pairs={{0,2},{1,3},{2,0},{3,1},{4,6},{5,7},{6,4},{7,5},{8,10},{9,11},{10,... | collective-permute-start | bytes 491528 | tf_op jit(solution)/shard_map/ppermute | solution.py:270
  16.2 1.0 %collective-permute-done.5.other_ref = bf16[9,64,128]{2,1,0:T(8,128)(2,1)S(1)} collective-permute-done((bf16[9,64,128]{2,1,0:T(8,128)(2,1)S(1)}, bf16[9,64,128]{2,1,0:T(8,128)(2,1)S(1)}, u32[]{:S(2)}, u32[]{:S(2)}) %collective-permute-start.5) | collective-permute-done | bytes 147488 | tf_op jit(solution)/shard_map/ppermute | solution.py:270
  17.2 0.2 cross_level.20.after_ref.own_ref
  17.5 1.6 %collective-permute-start.10 = (bf16[9,64,128]{2,1,0:T(8,128)(2,1)S(1)}, bf16[9,64,128]{2,1,0:T(8,128)(2,1)S(1)}, u32[]{:S(2)}, u32[]{:S(2)}) collective-permute-start(bf16[9,64,128]{2,1,0:T(8,128)(2,1)S(1)} %cross_level.20.after_ref.own_ref), channel_id=1, source_target_pairs={{0,4},{4,0},{8,12},{12,8},{16,20},{20,16},{24,28},{28,24},{1,5},{5... | collective-permute-start | bytes 442376 | tf_op jit(solution)/shard_map/ppermute | solution.py:270
  19.0 0.2 cross_level.21.after_ref.own_ref
  19.2 1.6 %collective-permute-start.9 = (bf16[4,64,128]{2,1,0:T(8,128)(2,1)S(1)}, bf16[4,64,128]{2,1,0:T(8,128)(2,1)S(1)}, u32[]{:S(2)}, u32[]{:S(2)}) collective-permute-start(bf16[4,64,128]{2,1,0:T(8,128)(2,1)S(1)} %cross_level.21.after_ref.own_ref), channel_id=1, source_target_pairs={{0,8},{4,12},{8,0},{12,4},{16,24},{20,28},{24,16},{28,20},{1,9},{5... | collective-permute-start | bytes 196616 | tf_op jit(solution)/shard_map/ppermute | solution.py:270
  20.9 0.2 cross_level.22.after_ref.own_ref
  21.1 0.6 %collective-permute-start.6 = (bf16[9,64,128]{2,1,0:T(8,128)(2,1)S(1)}, bf16[9,64,128]{2,1,0:T(8,128)(2,1)S(1)}, u32[]{:S(2)}, u32[]{:S(2)}) collective-permute-start(bf16[9,64,128]{2,1,0:T(8,128)(2,1)S(1)} %cross_level.22.after_ref.own_ref), channel_id=1, source_target_pairs={{0,2},{1,3},{2,0},{3,1},{4,6},{5,7},{6,4},{7,5},{8,10},{9,11},{10,... | collective-permute-start | bytes 442376 | tf_op jit(solution)/shard_map/ppermute | solution.py:270
  21.7 0.2 cross_level.23.after_ref.own_ref
  21.9 0.7 %collective-permute-start.8 = (bf16[10,64,128]{2,1,0:T(8,128)(2,1)S(1)}, bf16[10,64,128]{2,1,0:T(8,128)(2,1)S(1)}, u32[]{:S(2)}, u32[]{:S(2)}) collective-permute-start(bf16[10,64,128]{2,1,0:T(8,128)(2,1)S(1)} %cross_level.23.after_ref.own_ref), channel_id=1, source_target_pairs={{0,4},{4,0},{8,12},{12,8},{16,20},{20,16},{24,28},{28,24},{1,5},{5... | collective-permute-start | bytes 491528 | tf_op jit(solution)/shard_map/ppermute | solution.py:270
  22.6 0.1 collective-permute-done.10.other_ref
  22.7 0.2 cross_level.24.after_ref.own_ref
  22.9 1.8 %collective-permute-start.12 = (bf16[9,64,128]{2,1,0:T(8,128)(2,1)S(1)}, bf16[9,64,128]{2,1,0:T(8,128)(2,1)S(1)}, u32[]{:S(2)}, u32[]{:S(2)}) collective-permute-start(bf16[9,64,128]{2,1,0:T(8,128)(2,1)S(1)} %cross_level.24.after_ref.own_ref), channel_id=1, source_target_pairs={{0,8},{4,12},{8,0},{12,4},{16,24},{20,28},{24,16},{28,20},{1,9},{5... | collective-permute-start | bytes 442376 | tf_op jit(solution)/shard_map/ppermute | solution.py:270
  24.7 0.2 cross_level.25.after_ref.own_ref
  24.9 2.6 %collective-permute-start.18 = (bf16[4,64,128]{2,1,0:T(8,128)(2,1)S(1)}, bf16[4,64,128]{2,1,0:T(8,128)(2,1)S(1)}, u32[]{:S(2)}, u32[]{:S(2)}) collective-permute-start(bf16[4,64,128]{2,1,0:T(8,128)(2,1)S(1)} %cross_level.25.after_ref.own_ref), channel_id=1, source_target_pairs={{0,16},{4,20},{8,24},{12,28},{16,0},{20,4},{24,8},{28,12},{1,17},{... | collective-permute-start | bytes 196616 | tf_op jit(solution)/shard_map/ppermute | solution.py:270
  27.5 0.2 cross_level.26.after_ref.own_ref
  27.8 0.5 collective-permute-start.14
  28.3 0.2 cross_level.27.after_ref.own_ref
  28.5 1.4 %collective-permute-start.11 = (bf16[9,64,128]{2,1,0:T(8,128)(2,1)S(1)}, bf16[9,64,128]{2,1,0:T(8,128)(2,1)S(1)}, u32[]{:S(2)}, u32[]{:S(2)}) collective-permute-start(bf16[9,64,128]{2,1,0:T(8,128)(2,1)S(1)} %cross_level.27.after_ref.own_ref), channel_id=1, source_target_pairs={{0,4},{4,0},{8,12},{12,8},{16,20},{20,16},{24,28},{28,24},{1,5},{5... | collective-permute-start | bytes 442376 | tf_op jit(solution)/shard_map/ppermute | solution.py:270
  30.0 0.2 cross_level.28.after_ref.own_ref
  30.2 2.7 %collective-permute-start.17 = (bf16[9,64,128]{2,1,0:T(8,128)(2,1)S(1)}, bf16[9,64,128]{2,1,0:T(8,128)(2,1)S(1)}, u32[]{:S(2)}, u32[]{:S(2)}) collective-permute-start(bf16[9,64,128]{2,1,0:T(8,128)(2,1)S(1)} %cross_level.28.after_ref.own_ref), channel_id=1, source_target_pairs={{0,16},{4,20},{8,24},{12,28},{16,0},{20,4},{24,8},{28,12},{1,17},{... | collective-permute-start | bytes 442376 | tf_op jit(solution)/shard_map/ppermute | solution.py:270
  32.9 0.9 %collective-permute-done.11.other_ref = bf16[9,64,128]{2,1,0:T(8,128)(2,1)S(1)} collective-permute-done((bf16[9,64,128]{2,1,0:T(8,128)(2,1)S(1)}, bf16[9,64,128]{2,1,0:T(8,128)(2,1)S(1)}, u32[]{:S(2)}, u32[]{:S(2)}) %collective-permute-start.11) | collective-permute-done | bytes 147488 | tf_op jit(solution)/shard_map/ppermute | solution.py:270
  33.7 0.2 cross_level.29.after_ref.own_ref
  34.0 1.6 %collective-permute-start.13 = (bf16[9,64,128]{2,1,0:T(8,128)(2,1)S(1)}, bf16[9,64,128]{2,1,0:T(8,128)(2,1)S(1)}, u32[]{:S(2)}, u32[]{:S(2)}) collective-permute-start(bf16[9,64,128]{2,1,0:T(8,128)(2,1)S(1)} %cross_level.29.after_ref.own_ref), channel_id=1, source_target_pairs={{0,8},{4,12},{8,0},{12,4},{16,24},{20,28},{24,16},{28,20},{1,9},{5... | collective-permute-start | bytes 442376 | tf_op jit(solution)/shard_map/ppermute | solution.py:270
  35.6 0.2 cross_level.30.after_ref.own_ref
  35.9 2.4 %collective-permute-start.16 = (bf16[10,64,128]{2,1,0:T(8,128)(2,1)S(1)}, bf16[10,64,128]{2,1,0:T(8,128)(2,1)S(1)}, u32[]{:S(2)}, u32[]{:S(2)}) collective-permute-start(bf16[10,64,128]{2,1,0:T(8,128)(2,1)S(1)} %cross_level.30.after_ref.own_ref), channel_id=1, source_target_pairs={{0,16},{4,20},{8,24},{12,28},{16,0},{20,4},{24,8},{28,12},{1,17},{... | collective-permute-start | bytes 491528 | tf_op jit(solution)/shard_map/ppermute | solution.py:270
  38.3 2.6 %collective-permute-done.13.other_ref = bf16[9,64,128]{2,1,0:T(8,128)(2,1)S(1)} collective-permute-done((bf16[9,64,128]{2,1,0:T(8,128)(2,1)S(1)}, bf16[9,64,128]{2,1,0:T(8,128)(2,1)S(1)}, u32[]{:S(2)}, u32[]{:S(2)}) %collective-permute-start.13) | collective-permute-done | bytes 147488 | tf_op jit(solution)/shard_map/ppermute | solution.py:270
  40.9 0.2 cross_level.31.rest_0_.own_ref
  41.2 2.2 %collective-permute-start.15 = (bf16[9,64,128]{2,1,0:T(8,128)(2,1)S(1)}, bf16[9,64,128]{2,1,0:T(8,128)(2,1)S(1)}, u32[]{:S(2)}, u32[]{:S(2)}) collective-permute-start(bf16[9,64,128]{2,1,0:T(8,128)(2,1)S(1)} %cross_level.31.rest_0_.own_ref), channel_id=1, source_target_pairs={{0,16},{4,20},{8,24},{12,28},{16,0},{20,4},{24,8},{28,12},{1,17},{... | collective-permute-start | bytes 442376 | tf_op jit(solution)/shard_map/ppermute | solution.py:270
  43.3 1.1 %final_level.4 = (bf16[64,16384]{1,0:T(8,128)(2,1)}, f32[8,128]{1,0:T(8,128)S(1)}) custom-call(bf16[4,64,128]{2,1,0:T(8,128)(2,1)S(1)} %cross_level.25.after_ref.own_ref, bf16[4,64,128]{2,1,0:T(8,128)(2,1)S(1)} %collective-permute-done.18.other_ref, bf16[64,3,64,128]{3,2,1,0:T(8,128)(2,1)S(1)} %copy-done.1, bf16[64,64,256]{2,1,0:T(8,128)(2,1)S(1)} %copy-done.2, ...), custom_call_target="tpu_custom_call" | custom-call | flops 3000000000 | tf_op jit(solution)/shard_map/final_level/pallas_call | solution.py:249
  44.4 1.3 %final_level.5 = (bf16[64,16384]{1,0:T(8,128)(2,1)}, f32[8,128]{1,0:T(8,128)S(1)}) custom-call(bf16[9,64,128]{2,1,0:T(8,128)(2,1)S(1)} %cross_level.28.after_ref.own_ref, bf16[9,64,128]{2,1,0:T(8,128)(2,1)S(1)} %collective-permute-done.17.other_ref, bf16[64,3,64,128]{3,2,1,0:T(8,128)(2,1)S(1)} %copy-done.1, ...), custom_call_target="tpu_custom_call", output_to_operand_aliasing={{0}: (5, {})} | custom-call | flops 3000000000 | tf_op jit(solution)/shard_map/final_level/pallas_call | solution.py:249
  45.7 4.0 %collective-permute-done.16.other_ref = bf16[10,64,128]{2,1,0:T(8,128)(2,1)S(1)} collective-permute-done((bf16[10,64,128]{2,1,0:T(8,128)(2,1)S(1)}, bf16[10,64,128]{2,1,0:T(8,128)(2,1)S(1)}, u32[]{:S(2)}, u32[]{:S(2)}) %collective-permute-start.16) | collective-permute-done | bytes 163872 | tf_op jit(solution)/shard_map/ppermute | solution.py:270
  49.7 1.3 %final_level.6 = (bf16[64,16384]{1,0:T(8,128)(2,1)}, f32[8,128]{1,0:T(8,128)S(1)}) custom-call(bf16[10,64,128]{2,1,0:T(8,128)(2,1)S(1)} %cross_level.30.after_ref.own_ref, bf16[10,64,128]{2,1,0:T(8,128)(2,1)S(1)} %collective-permute-done.16.other_ref, bf16[64,3,64,128]{3,2,1,0:T(8,128)(2,1)S(1)} %copy-done.1, ...), custom_call_target="tpu_custom_call", output_to_operand_aliasing={{0}: (5, {})} | custom-call | flops 3000000000 | tf_op jit(solution)/shard_map/final_level/pallas_call | solution.py:249
  51.0 0.7 %collective-permute-done.15.other_ref = bf16[9,64,128]{2,1,0:T(8,128)(2,1)S(1)} collective-permute-done((bf16[9,64,128]{2,1,0:T(8,128)(2,1)S(1)}, bf16[9,64,128]{2,1,0:T(8,128)(2,1)S(1)}, u32[]{:S(2)}, u32[]{:S(2)}) %collective-permute-start.15) | collective-permute-done | bytes 147488 | tf_op jit(solution)/shard_map/ppermute | solution.py:270
  51.7 1.3 %final_level.7 = bf16[64,16384]{1,0:T(8,128)(2,1)} custom-call(bf16[9,64,128]{2,1,0:T(8,128)(2,1)S(1)} %cross_level.31.rest_0_.own_ref, bf16[9,64,128]{2,1,0:T(8,128)(2,1)S(1)} %collective-permute-done.15.other_ref, bf16[64,3,64,128]{3,2,1,0:T(8,128)(2,1)S(1)} %copy-done.1, bf16[64,64,256]{2,1,0:T(8,128)(2,1)S(1)} %copy-done.2, ...), custom_call_target="tpu_custom_call", output_to_operand_aliasing={{}: (5, {})} | custom-call | flops 3000000000 | tf_op jit(solution)/shard_map/final_level/pallas_call | solution.py:249
  (18 shorter events, 0.1 us)
Async XLA Ops:
  5.3 1.4 %collective-permute-start.1 = (bf16[4,64,128]{2,1,0:T(8,128)(2,1)S(1)}, bf16[4,64,128]{2,1,0:T(8,128)(2,1)S(1)}, u32[]{:S(2)}, u32[]{:S(2)}) collective-permute-start(bf16[4,64,128]{2,1,0:T(8,128)(2,1)S(1)} %get-tuple-element.20.own_ref), channel_id=1, source_target_pairs={{0,1},{1,0},{2,3},{3,2},{4,5},{5,4},{6,7},{7,6},{8,9},{9,8},{10,11... | collective-permute-start | bytes 196616 | tf_op jit(solution)/shard_map/ppermute | solution.py:270
  5.9 4.0 %collective-permute-start = (bf16[9,64,128]{2,1,0:T(8,128)(2,1)S(1)}, bf16[9,64,128]{2,1,0:T(8,128)(2,1)S(1)}, u32[]{:S(2)}, u32[]{:S(2)}) collective-permute-start(bf16[9,64,128]{2,1,0:T(8,128)(2,1)S(1)} %get-tuple-element.18.own_ref), channel_id=1, source_target_pairs={{0,1},{1,0},{2,3},{3,2},{4,5},{5,4},{6,7},{7,6},{8,9},{9,8},{10,11... | collective-permute-start | bytes 442376 | tf_op jit(solution)/shard_map/ppermute | solution.py:270
  6.9 5.3 %collective-permute-start.3 = (bf16[4,64,128]{2,1,0:T(8,128)(2,1)S(1)}, bf16[4,64,128]{2,1,0:T(8,128)(2,1)S(1)}, u32[]{:S(2)}, u32[]{:S(2)}) collective-permute-start(bf16[4,64,128]{2,1,0:T(8,128)(2,1)S(1)} %cross_level.16.after_ref.own_ref), channel_id=1, source_target_pairs={{0,2},{1,3},{2,0},{3,1},{4,6},{5,7},{6,4},{7,5},{8,10},{9,11},{10,... | collective-permute-start | bytes 196616 | tf_op jit(solution)/shard_map/ppermute | solution.py:270
  10.1 2.2 %copy-start = (bf16[64,2,64,128]{3,2,1,0:T(8,128)(2,1)S(1)}, bf16[64,2,64,128]{3,2,1,0:T(8,128)(2,1)}, u32[]{:S(2)}) copy-start(bf16[64,2,64,128]{3,2,1,0:T(8,128)(2,1)} %mix_ref.27) | copy-start | bytes 6291460
  10.4 3.9 %collective-permute-start.2 = (bf16[19,64,128]{2,1,0:T(8,128)(2,1)S(1)}, bf16[19,64,128]{2,1,0:T(8,128)(2,1)S(1)}, u32[]{:S(2)}, u32[]{:S(2)}) collective-permute-start(bf16[19,64,128]{2,1,0:T(8,128)(2,1)S(1)} %local_rest.1.after_ref.own_ref), channel_id=1, source_target_pairs={{0,1},{1,0},{2,3},{3,2},{4,5},{5,4},{6,7},{7,6},{8,9},{9,8},{10,11... | collective-permute-start | bytes 933896 | tf_op jit(solution)/shard_map/ppermute | solution.py:270
  10.5 6.7 %collective-permute-start.5 = (bf16[9,64,128]{2,1,0:T(8,128)(2,1)S(1)}, bf16[9,64,128]{2,1,0:T(8,128)(2,1)S(1)}, u32[]{:S(2)}, u32[]{:S(2)}) collective-permute-start(bf16[9,64,128]{2,1,0:T(8,128)(2,1)S(1)} %cross_level.17.after_ref.own_ref), channel_id=1, source_target_pairs={{0,2},{1,3},{2,0},{3,1},{4,6},{5,7},{6,4},{7,5},{8,10},{9,11},{10,... | collective-permute-start | bytes 442376 | tf_op jit(solution)/shard_map/ppermute | solution.py:270
  12.5 6.6 %collective-permute-start.4 = (bf16[4,64,128]{2,1,0:T(8,128)(2,1)S(1)}, bf16[4,64,128]{2,1,0:T(8,128)(2,1)S(1)}, u32[]{:S(2)}, u32[]{:S(2)}) collective-permute-start(bf16[4,64,128]{2,1,0:T(8,128)(2,1)S(1)} %cross_level.18.after_ref.own_ref), channel_id=1, source_target_pairs={{0,4},{4,0},{8,12},{12,8},{16,20},{20,16},{24,28},{28,24},{1,5},{5... | collective-permute-start | bytes 196616 | tf_op jit(solution)/shard_map/ppermute | solution.py:270
  14.6 4.4 %copy-start.1 = (bf16[64,3,64,128]{3,2,1,0:T(8,128)(2,1)S(1)}, bf16[64,3,64,128]{3,2,1,0:T(8,128)(2,1)}, u32[]{:S(2)}) copy-start(bf16[64,3,64,128]{3,2,1,0:T(8,128)(2,1)} %mix_ref.35) | copy-start | bytes 9437188
  14.6 7.1 %collective-permute-start.7 = (bf16[10,64,128]{2,1,0:T(8,128)(2,1)S(1)}, bf16[10,64,128]{2,1,0:T(8,128)(2,1)S(1)}, u32[]{:S(2)}, u32[]{:S(2)}) collective-permute-start(bf16[10,64,128]{2,1,0:T(8,128)(2,1)S(1)} %cross_level.19.after_ref.own_ref), channel_id=1, source_target_pairs={{0,2},{1,3},{2,0},{3,1},{4,6},{5,7},{6,4},{7,5},{8,10},{9,11},{10,... | collective-permute-start | bytes 491528 | tf_op jit(solution)/shard_map/ppermute | solution.py:270
  17.5 5.2 %collective-permute-start.10 = (bf16[9,64,128]{2,1,0:T(8,128)(2,1)S(1)}, bf16[9,64,128]{2,1,0:T(8,128)(2,1)S(1)}, u32[]{:S(2)}, u32[]{:S(2)}) collective-permute-start(bf16[9,64,128]{2,1,0:T(8,128)(2,1)S(1)} %cross_level.20.after_ref.own_ref), channel_id=1, source_target_pairs={{0,4},{4,0},{8,12},{12,8},{16,20},{20,16},{24,28},{28,24},{1,5},{5... | collective-permute-start | bytes 442376 | tf_op jit(solution)/shard_map/ppermute | solution.py:270
  19.2 5.5 %collective-permute-start.9 = (bf16[4,64,128]{2,1,0:T(8,128)(2,1)S(1)}, bf16[4,64,128]{2,1,0:T(8,128)(2,1)S(1)}, u32[]{:S(2)}, u32[]{:S(2)}) collective-permute-start(bf16[4,64,128]{2,1,0:T(8,128)(2,1)S(1)} %cross_level.21.after_ref.own_ref), channel_id=1, source_target_pairs={{0,8},{4,12},{8,0},{12,4},{16,24},{20,28},{24,16},{28,20},{1,9},{5... | collective-permute-start | bytes 196616 | tf_op jit(solution)/shard_map/ppermute | solution.py:270
  21.1 7.2 %collective-permute-start.6 = (bf16[9,64,128]{2,1,0:T(8,128)(2,1)S(1)}, bf16[9,64,128]{2,1,0:T(8,128)(2,1)S(1)}, u32[]{:S(2)}, u32[]{:S(2)}) collective-permute-start(bf16[9,64,128]{2,1,0:T(8,128)(2,1)S(1)} %cross_level.22.after_ref.own_ref), channel_id=1, source_target_pairs={{0,2},{1,3},{2,0},{3,1},{4,6},{5,7},{6,4},{7,5},{8,10},{9,11},{10,... | collective-permute-start | bytes 442376 | tf_op jit(solution)/shard_map/ppermute | solution.py:270
  21.9 5.6 %collective-permute-start.8 = (bf16[10,64,128]{2,1,0:T(8,128)(2,1)S(1)}, bf16[10,64,128]{2,1,0:T(8,128)(2,1)S(1)}, u32[]{:S(2)}, u32[]{:S(2)}) collective-permute-start(bf16[10,64,128]{2,1,0:T(8,128)(2,1)S(1)} %cross_level.23.after_ref.own_ref), channel_id=1, source_target_pairs={{0,4},{4,0},{8,12},{12,8},{16,20},{20,16},{24,28},{28,24},{1,5},{5... | collective-permute-start | bytes 491528 | tf_op jit(solution)/shard_map/ppermute | solution.py:270
  22.9 7.0 %collective-permute-start.12 = (bf16[9,64,128]{2,1,0:T(8,128)(2,1)S(1)}, bf16[9,64,128]{2,1,0:T(8,128)(2,1)S(1)}, u32[]{:S(2)}, u32[]{:S(2)}) collective-permute-start(bf16[9,64,128]{2,1,0:T(8,128)(2,1)S(1)} %cross_level.24.after_ref.own_ref), channel_id=1, source_target_pairs={{0,8},{4,12},{8,0},{12,4},{16,24},{20,28},{24,16},{28,20},{1,9},{5... | collective-permute-start | bytes 442376 | tf_op jit(solution)/shard_map/ppermute | solution.py:270
  24.9 18.4 %collective-permute-start.18 = (bf16[4,64,128]{2,1,0:T(8,128)(2,1)S(1)}, bf16[4,64,128]{2,1,0:T(8,128)(2,1)S(1)}, u32[]{:S(2)}, u32[]{:S(2)}) collective-permute-start(bf16[4,64,128]{2,1,0:T(8,128)(2,1)S(1)} %cross_level.25.after_ref.own_ref), channel_id=1, source_target_pairs={{0,16},{4,20},{8,24},{12,28},{16,0},{20,4},{24,8},{28,12},{1,17},{... | collective-permute-start | bytes 196616 | tf_op jit(solution)/shard_map/ppermute | solution.py:270
  27.8 7.8 %collective-permute-start.14 = (bf16[10,64,128]{2,1,0:T(8,128)(2,1)S(1)}, bf16[10,64,128]{2,1,0:T(8,128)(2,1)S(1)}, u32[]{:S(2)}, u32[]{:S(2)}) collective-permute-start(bf16[10,64,128]{2,1,0:T(8,128)(2,1)S(1)} %cross_level.26.after_ref.own_ref), channel_id=1, source_target_pairs={{0,8},{4,12},{8,0},{12,4},{16,24},{20,28},{24,16},{28,20},{1,9},{5... | collective-permute-start | bytes 491528 | tf_op jit(solution)/shard_map/ppermute | solution.py:270
  28.5 5.2 %collective-permute-start.11 = (bf16[9,64,128]{2,1,0:T(8,128)(2,1)S(1)}, bf16[9,64,128]{2,1,0:T(8,128)(2,1)S(1)}, u32[]{:S(2)}, u32[]{:S(2)}) collective-permute-start(bf16[9,64,128]{2,1,0:T(8,128)(2,1)S(1)} %cross_level.27.after_ref.own_ref), channel_id=1, source_target_pairs={{0,4},{4,0},{8,12},{12,8},{16,20},{20,16},{24,28},{28,24},{1,5},{5... | collective-permute-start | bytes 442376 | tf_op jit(solution)/shard_map/ppermute | solution.py:270
  30.2 14.2 %collective-permute-start.17 = (bf16[9,64,128]{2,1,0:T(8,128)(2,1)S(1)}, bf16[9,64,128]{2,1,0:T(8,128)(2,1)S(1)}, u32[]{:S(2)}, u32[]{:S(2)}) collective-permute-start(bf16[9,64,128]{2,1,0:T(8,128)(2,1)S(1)} %cross_level.28.after_ref.own_ref), channel_id=1, source_target_pairs={{0,16},{4,20},{8,24},{12,28},{16,0},{20,4},{24,8},{28,12},{1,17},{... | collective-permute-start | bytes 442376 | tf_op jit(solution)/shard_map/ppermute | solution.py:270
  34.0 7.0 %collective-permute-start.13 = (bf16[9,64,128]{2,1,0:T(8,128)(2,1)S(1)}, bf16[9,64,128]{2,1,0:T(8,128)(2,1)S(1)}, u32[]{:S(2)}, u32[]{:S(2)}) collective-permute-start(bf16[9,64,128]{2,1,0:T(8,128)(2,1)S(1)} %cross_level.29.after_ref.own_ref), channel_id=1, source_target_pairs={{0,8},{4,12},{8,0},{12,4},{16,24},{20,28},{24,16},{28,20},{1,9},{5... | collective-permute-start | bytes 442376 | tf_op jit(solution)/shard_map/ppermute | solution.py:270
  35.9 7.5 %copy-start.2 = (bf16[64,64,256]{2,1,0:T(8,128)(2,1)S(1)}, bf16[64,64,256]{2,1,0:T(8,128)(2,1)}, u32[]{:S(2)}) copy-start(bf16[64,64,256]{2,1,0:T(8,128)(2,1)} %leaf_ref.7) | copy-start | bytes 6291460
  35.9 13.8 %collective-permute-start.16 = (bf16[10,64,128]{2,1,0:T(8,128)(2,1)S(1)}, bf16[10,64,128]{2,1,0:T(8,128)(2,1)S(1)}, u32[]{:S(2)}, u32[]{:S(2)}) collective-permute-start(bf16[10,64,128]{2,1,0:T(8,128)(2,1)S(1)} %cross_level.30.after_ref.own_ref), channel_id=1, source_target_pairs={{0,16},{4,20},{8,24},{12,28},{16,0},{20,4},{24,8},{28,12},{1,17},{... | collective-permute-start | bytes 491528 | tf_op jit(solution)/shard_map/ppermute | solution.py:270
  41.2 10.6 %collective-permute-start.15 = (bf16[9,64,128]{2,1,0:T(8,128)(2,1)S(1)}, bf16[9,64,128]{2,1,0:T(8,128)(2,1)S(1)}, u32[]{:S(2)}, u32[]{:S(2)}) collective-permute-start(bf16[9,64,128]{2,1,0:T(8,128)(2,1)S(1)} %cross_level.31.rest_0_.own_ref), channel_id=1, source_target_pairs={{0,16},{4,20},{8,24},{12,28},{16,0},{20,4},{24,8},{28,12},{1,17},{... | collective-permute-start | bytes 442376 | tf_op jit(solution)/shard_map/ppermute | solution.py:270
